TPU v7x, 32 devices: a whole 2x2x4 slice. The times are simulated.
32 devices in a mesh: basis: 16 (over z, y, core), state: 2 (over x).
Axes of the slice: x: 2, y: 2, z: 4, core: 2. Of those that a mesh axis runs over, the one named last changes fastest.
Arguments:
- vectors: bfloat16 [512, 81920], P('state', 'basis'), may hold values from -6 to 6
- blocks: bfloat16 [640, 18, 128, 128], P('basis', 'state'), may hold values from -0.125 to 0.125
- columns: int32 [640, 18], P('basis', 'state'), may hold values from 0 to 639, as said below
- counts: int32 [640], P('basis'), may hold values from 4 to 18, as said below
Outputs:
- sigma: bfloat16 [512, 81920], P('state', 'basis')
Inputs may be any that keep to these rules, and one draw needn't show every extreme that they name: Every block column lies within 36 blocks of its block row and inside the basis; a row's slots name distinct columns except near the basis ends, where a column may repeat. Slots k < counts[r] are live; some block row has all 18 slots live.
All inputs are finite; a program needn't handle non-finite values.
Results may differ from a plain program's by a relative error of at most 0.001.
Values may be sent and summed in bfloat16 or wider, within the bound.
No kernel may reach another device: no remote copies, remote signals or barrier semaphores. Data moves between devices by JAX's collectives and lax.ppermute only.
A program may use at most 192 MiB of HBM per device.

v0:
```python
import functools
import math

import jax
import jax.numpy as jnp
from jax import lax
from jax.experimental import pallas as pl
from jax.experimental.pallas import tpu as pltpu
from jax.sharding import PartitionSpec as P

W = 36
VMEM_LIMIT = 32 * 1024 * 1024
TOP = 32767.0
FINE = 65536.0
SMALLEST = 2.0**-100


def after(array, *others):
    return lax.optimization_barrier((array, *others))[0]


def fill(sources, plan, ext):
    at, step = 0, 16
    for part, (start, size, _) in enumerate(plan):
        left, own, right = sources[3 * part : 3 * part + 3]
        reach, width = left.shape[1], own.shape[1]

        @pl.loop(0, size // step)
        def _(i, left=left, own=own, right=right, start=start, at=at, reach=reach, width=width):
            here = pl.ds(pl.multiple_of(i * step, step), step)
            mine = pl.ds(pl.multiple_of(start + i * step, step), step)
            to = pl.ds(pl.multiple_of(at + i * step, step), step)
            ext[to, :reach] = left[here, :]
            ext[to, reach : reach + width] = own[mine, :]
            ext[to, reach + width : 2 * reach + width] = right[here, :]

        at += size


def row_sums(index_ref, row, slots, block, ext, panel_ref):
    picked = jnp.concatenate(
        [
            ext[:, pl.ds(pl.multiple_of(index_ref[row * slots + slot] * block, block), block)]
            for slot in range(slots)
        ],
        axis=1,
    )
    panel = jnp.concatenate([panel_ref[slot] for slot in range(slots)], axis=1)
    return lax.dot_general(
        picked, panel, (((1,), (1,)), ((), ())), preferred_element_type=jnp.float32
    )


def level_code(top):
    return jnp.ceil(jnp.log2(jnp.maximum(top, SMALLEST)) * FINE).astype(jnp.int32)


def level_of(code):
    return jnp.exp2(code.astype(jnp.float32) * (1.0 / FINE))


def code_into(out_ref, first, block, words, sums):
    lane = lax.broadcasted_iota(jnp.int32, (out_ref.shape[0], block), 1)
    codes = out_ref[:, words * block :]
    values = []
    for member, mine in enumerate(sums):
        code = level_code(jnp.max(jnp.abs(mine), axis=1, keepdims=True))
        codes = jnp.where(lane == first + member, code, codes)
        scaled = jnp.round(mine * (TOP / level_of(code)))
        values.append(jnp.clip(scaled, -TOP, TOP).astype(jnp.int32))
    out_ref[:, words * block :] = codes
    for pair in range(len(sums) // 2):
        word = (values[2 * pair + 1] << 16) | (values[2 * pair] & 0xFFFF)
        at = pl.multiple_of((first // 2 + pair) * block, block)
        out_ref[:, pl.ds(at, block)] = word


def products_kernel(plan, group, slots, block, words, index_ref, *refs):
    parts = len(plan)
    sources, blocks_ref = refs[: 3 * parts], refs[3 * parts]
    outs, (ext, panels, panel_sems) = refs[3 * parts + 1 : 4 * parts + 1], refs[4 * parts + 1 :]
    rows, pieces = panels.shape[0], panel_sems.shape[0]
    piece = rows // pieces

    def panel_copy(n):
        here = pl.ds(n * piece, piece)
        return pltpu.make_async_copy(blocks_ref.at[here], panels.at[here], panel_sems.at[n])

    for n in range(pieces):
        panel_copy(n).start()
    fill(sources, plan, ext)
    end = ext.shape[1] - block
    ext[:, end:] = jnp.zeros((ext.shape[0], block), ext.dtype)
    for (_, size, coded), out_ref in zip(plan, outs):
        if coded:
            out_ref[:, words * block :] = jnp.zeros((size, block), jnp.int32)

    @pl.loop(0, rows // group)
    def _(step):
        for n in range(group // piece):
            panel_copy(step * (group // piece) + n).wait()
        first = step * group
        sums = [
            row_sums(index_ref, first + member, slots, block, ext, panels.at[first + member])
            for member in range(group)
        ]
        at = 0
        for (_, size, coded), out_ref in zip(plan, outs):
            mine = [total[at : at + size] for total in sums]
            if coded:
                code_into(out_ref, first, block, words, mine)
            else:
                for member in range(group):
                    column = pl.multiple_of((first + member) * block, block)
                    out_ref[:, pl.ds(column, block)] = mine[member]
            at += size


def products(index, parts, blocks):
    rows, slots, block, _ = blocks.shape
    reach, width = parts[0][0].shape[1], parts[0][1].shape[1]
    plan = tuple(part[3:] for part in parts)
    states = sum(size for _, size, _ in plan)
    group, words = 8 if rows % 8 == 0 else 2, rows // 2
    sources = [array for part in parts for array in part[:3]]
    in_vmem = pl.BlockSpec(memory_space=pltpu.VMEM)
    out_shape = []
    for _, size, coded in plan:
        if coded:
            out_shape.append(jax.ShapeDtypeStruct((size, (words + 1) * block), jnp.int32))
        else:
            out_shape.append(jax.ShapeDtypeStruct((size, width), jnp.float32))
    return pl.pallas_call(
        functools.partial(products_kernel, plan, group, slots, block, words),
        out_shape=out_shape,
        in_specs=[pl.BlockSpec(memory_space=pltpu.SMEM)]
        + [in_vmem] * len(sources)
        + [pl.BlockSpec(memory_space=pltpu.HBM)],
        out_specs=[in_vmem] * len(plan),
        scratch_shapes=[
            pltpu.VMEM((states, 2 * reach + width + block), parts[0][1].dtype),
            pltpu.VMEM(blocks.shape, blocks.dtype),
            pltpu.SemaphoreType.DMA((rows // 2,)),
        ],
        compiler_params=pltpu.CompilerParams(vmem_limit_bytes=VMEM_LIMIT),
        cost_estimate=pl.CostEstimate(flops=1, bytes_accessed=1, transcendentals=0),
        name="products",
    )(index, *sources, pltpu.with_memory_space_constraint(blocks, pltpu.HBM))


def finish_kernel(partials, block, pairs, own_ref, *refs):
    out_ref = refs[-1]
    step = pl.program_id(0)
    lane = lax.broadcasted_iota(jnp.int32, (own_ref.shape[0], block), 1)
    levels = [level_of(refs[2 * p + 1][...]) * (1.0 / TOP) for p in range(partials)]
    for pair in range(pairs):
        for half in range(2):
            at = (2 * pair + half) * block
            row = (step * pairs + pair) * 2 + half
            total = own_ref[:, at : at + block]
            for p in range(partials):
                word = refs[2 * p][:, pair * block : (pair + 1) * block]
                value = (word >> 16) if half else ((word << 16) >> 16)
                level = jnp.max(jnp.where(lane == row, levels[p], 0.0), axis=1, keepdims=True)
                total = total + value.astype(jnp.float32) * level
            out_ref[:, at : at + block] = total.astype(out_ref.dtype)


def finish(own_sums, own_start, coded, coded_start, out, start, size, states, block):
    width = own_sums.shape[1]
    words = width // block // 2
    pairs = words // 2 if words % 2 == 0 else 1
    rows, wide, narrow = pl.Element(size), pl.Element(2 * pairs * block), pl.Element(pairs * block)
    own_at, coded_at = start - own_start, start - coded_start
    in_specs = [pl.BlockSpec((rows, wide), lambda i: (own_at, i * 2 * pairs * block))]
    operands = [own_sums]
    for array in coded:
        in_specs.append(pl.BlockSpec((rows, narrow), lambda i: (coded_at, i * pairs * block)))
        in_specs.append(pl.BlockSpec((rows, pl.Element(block)), lambda i: (coded_at, words * block)))
        operands += [array, array]
    aliases = {}
    if out is not None:
        aliases = {len(operands): 0}
        in_specs.append(pl.BlockSpec(memory_space=pl.ANY))
        operands.append(out)
    return pl.pallas_call(
        functools.partial(finish_kernel, len(coded), block, pairs),
        out_shape=jax.ShapeDtypeStruct((states, width), jnp.bfloat16),
        grid=(words // pairs,),
        in_specs=in_specs,
        out_specs=pl.BlockSpec((rows, wide), lambda i: (start, i * 2 * pairs * block)),
        input_output_aliases=aliases,
        compiler_params=pltpu.CompilerParams(vmem_limit_bytes=VMEM_LIMIT),
        cost_estimate=pl.CostEstimate(flops=1, bytes_accessed=1, transcendentals=0),
        name="finish",
    )(*operands)


def starts_of(sizes):
    return [sum(sizes[:i]) for i in range(len(sizes))]


def on_device(vectors, blocks, columns, counts):
    states, width = vectors.shape
    rows, slots, block, _ = blocks.shape
    reach = W * block
    basis_size, state_size = lax.axis_size("basis"), lax.axis_size("state")
    if states % 256 == 0:
        sizes = (5 * states // 16, 3 * states // 8, 5 * states // 16)
        own_sizes = (7 * states // 16, 9 * states // 16)
    else:
        sizes, own_sizes = (states,), (states,)
    starts, own_starts = starts_of(sizes), starts_of(own_sizes)

    slot_index = lax.axis_index("state") * slots + jnp.arange(slots, dtype=jnp.int32)
    relative = columns - (lax.axis_index("basis") * rows - W)
    zeros_at = rows + 2 * W
    index = jnp.where(slot_index[None, :] < counts[:, None], relative, zeros_at).reshape(-1)

    up = [(i, i + 1) for i in range(basis_size - 1)]
    down = [(i + 1, i) for i in range(basis_size - 1)]

    def edges_of(piece, *others):
        edges = (piece[:, width - reach :], piece[:, :reach])
        return lax.optimization_barrier((*edges, *others))[:2] if others else edges

    def halo(edges):
        return lax.ppermute(edges[0], "basis", up), lax.ppermute(edges[1], "basis", down)

    def shifted(piece, shift):
        return lax.ppermute(piece, "state", [(i, (i + shift) % state_size) for i in range(state_size)])

    def own_edges(part, *others):
        return edges_of(vectors[own_starts[part] : own_starts[part] + own_sizes[part]], *others)

    def own_part(part, ends):
        return (ends[0], vectors, ends[1], own_starts[part], own_sizes[part], False)

    def their_part(n):
        return (ends[n][0], theirs[n], ends[n][1], 0, theirs[n].shape[0], True)

    messages = [(shift, c) for shift in range(1, state_size) for c in range(len(sizes))]
    count = len(messages)
    theirs, edges, ends, sent, own_sums, received = [], [], [], [], [], []
    first_edges = own_edges(0)
    first = halo(first_edges)
    for n, (shift, c) in enumerate(messages):
        source = after(vectors, *(first_edges[::-1] if n == 1 else first)) if n else vectors
        theirs.append(shifted(source[starts[c] : starts[c] + sizes[c]], shift))

    def compute(n):
        later = (*edges[n + 1][:: -1 if n == 0 else 1], *edges[n][::-1]) if n + 1 < count else ()
        sent.extend(products(after(index, *later) if later else index, [their_part(n)], blocks))
        if n == 0:
            own_sums.extend(products(after(index, sent[0]), [own_part(0, first)], blocks))

    for n in range(count):
        edges.append(edges_of(theirs[n], *(own_sums if n > 1 else ())))
        ends.append(halo(edges[n]))
        if n:
            compute(n - 1)
    coded = [[] for _ in sizes]

    def send(n):
        shift, c = messages[n]
        message = after(sent[n], received[n - 1]) if n else sent[n]
        received.append(shifted(message, -shift))
        coded[c].append(received[n])

    def finish_piece(part, c, out):
        own_end, end = own_starts[part] + own_sizes[part], starts[c] + sizes[c]
        at, end = max(own_starts[part], starts[c]), min(own_end, end)
        if at >= end:
            return out
        return finish(
            own_sums[part], own_starts[part], coded[c], starts[c], out, at, end - at, states, block
        )

    out, done = None, set()
    if len(own_sizes) > 1:
        send(0)
        if state_size == 2:
            out = finish_piece(0, 0, out)
            done.add((0, 0))
        held = (out,) if done else ()
        last = halo(own_edges(1, *edges[-1], *sent[-1:], *held))
    compute(count - 1)
    for n in range(len(received), count):
        send(n)
    for part in range(len(own_sizes)):
        if part:
            own_sums += products(after(index, out), [own_part(part, last)], blocks)
        for c in range(len(sizes)):
            if (part, c) not in done:
                out = finish_piece(part, c, out)
    return out


def solution(mesh):
    in_specs = (
        P("state", "basis"),
        P("basis", "state", None, None),
        P("basis", "state"),
        P("basis"),
    )
    out_specs = P("state", "basis")
    return jax.shard_map(
        on_device, mesh=mesh, in_specs=in_specs, out_specs=out_specs, check_vma=False
    )
```

profile of v0, /device:TPU:9, one launch (start us, length us, event | category | flops | bytes accessed | tf_op | source)
XLA Modules:
  0.0 131.3 jit_solution(6732407677111103554)
XLA Ops:
  0.0 2.3 %slice.50 = bf16[80,5120]{1,0:T(8,128)(2,1)} slice(bf16[256,5120]{1,0:T(8,128)(2,1)} %refs_1_.3), slice={[0:80], [0:5120]} | slice | bytes 1638400 | tf_op jit(solution)/shard_map/slice | solution.py:249
  3.5 3.0 %fusion.1 = (bf16[112,4608]{1,0:T(8,128)(2,1)}, bf16[112,4608]{1,0:T(8,128)(2,1)}) fusion(bf16[256,5120]{1,0:T(8,128)(2,1)} %refs_1_.3), kind=kLoop, calls=%fused_computation.3 | loop fusion | bytes 4128768 | tf_op jit(solution)/shard_map/slice | solution.py:224
  6.5 4.0 %collective-permute-start.4 = (bf16[112,4608]{1,0:T(8,128)(2,1)}, bf16[112,4608]{1,0:T(8,128)(2,1)}, u32[]{:S(2)}, u32[]{:S(2)}) collective-permute-start(bf16[112,4608]{1,0:T(8,128)(2,1)} %get-tuple-element.31), channel_id=1, source_target_pairs={{0,2},{2,4},{4,6},{6,8},{8,10},{10,12},{12,14},{14,16},{16,18},{18... | collective-permute-start | bytes 3096584 | tf_op jit(solution)/shard_map/ppermute | solution.py:228
  10.5 1.9 %collective-permute-start.5 = (bf16[112,4608]{1,0:T(8,128)(2,1)}, bf16[112,4608]{1,0:T(8,128)(2,1)}, u32[]{:S(2)}, u32[]{:S(2)}) collective-permute-start(bf16[112,4608]{1,0:T(8,128)(2,1)} %get-tuple-element.32), channel_id=1, source_target_pairs={{2,0},{4,2},{6,4},{8,6},{10,8},{12,10},{14,12},{16,14},{18,16},{20... | collective-permute-start | bytes 3096584 | tf_op jit(solution)/shard_map/ppermute | solution.py:228
  14.0 7.7 %collective-permute-done.1.refs_1_ = bf16[80,5120]{1,0:T(8,128)(2,1)S(1)} collective-permute-done((bf16[80,5120]{1,0:T(8,128)(2,1)}, bf16[80,5120]{1,0:T(8,128)(2,1)S(1)}, u32[]{:S(2)}, u32[]{:S(2)}) %collective-permute-start.1) | collective-permute-done | bytes 819232 | tf_op jit(solution)/shard_map/ppermute | solution.py:231
  21.8 5.6 %collective-permute-start.2 = (bf16[80,4608]{1,0:T(8,128)(2,1)S(1)}, bf16[80,4608]{1,0:T(8,128)(2,1)S(1)}, u32[]{:S(2)}, u32[]{:S(2)}) collective-permute-start(bf16[80,4608]{1,0:T(8,128)(2,1)S(1)} %get-tuple-element.37), channel_id=1, source_target_pairs={{0,2},{2,4},{4,6},{6,8},{8,10},{10,12},{12,14},{14,16},{16,18},{18... | collective-permute-start | bytes 2211848 | tf_op jit(solution)/shard_map/ppermute | solution.py:228
  27.5 1.9 %collective-permute-start.3 = (bf16[80,4608]{1,0:T(8,128)(2,1)S(1)}, bf16[80,4608]{1,0:T(8,128)(2,1)S(1)}, u32[]{:S(2)}, u32[]{:S(2)}) collective-permute-start(bf16[80,4608]{1,0:T(8,128)(2,1)S(1)} %get-tuple-element.38), channel_id=1, source_target_pairs={{2,0},{4,2},{6,4},{8,6},{10,8},{12,10},{14,12},{16,14},{18,16},{20... | collective-permute-start | bytes 2211848 | tf_op jit(solution)/shard_map/ppermute | solution.py:228
  29.4 11.9 %collective-permute-done.4.refs_0_ = bf16[112,4608]{1,0:T(8,128)(2,1)} collective-permute-done((bf16[112,4608]{1,0:T(8,128)(2,1)}, bf16[112,4608]{1,0:T(8,128)(2,1)}, u32[]{:S(2)}, u32[]{:S(2)}) %collective-permute-start.4) | collective-permute-done | bytes 1032224 | tf_op jit(solution)/shard_map/ppermute | solution.py:228
  41.3 1.9 %collective-permute-done.5.refs_2_ = bf16[112,4608]{1,0:T(8,128)(2,1)} collective-permute-done((bf16[112,4608]{1,0:T(8,128)(2,1)}, bf16[112,4608]{1,0:T(8,128)(2,1)}, u32[]{:S(2)}, u32[]{:S(2)}) %collective-permute-start.5) | collective-permute-done | bytes 1032224 | tf_op jit(solution)/shard_map/ppermute | solution.py:228
  45.1 5.0 %collective-permute-start.7 = (bf16[96,4608]{1,0:T(8,128)(2,1)S(1)}, bf16[96,4608]{1,0:T(8,128)(2,1)S(1)}, u32[]{:S(2)}, u32[]{:S(2)}) collective-permute-start(bf16[96,4608]{1,0:T(8,128)(2,1)S(1)} %get-tuple-element.33), channel_id=1, source_target_pairs={{0,2},{2,4},{4,6},{6,8},{8,10},{10,12},{12,14},{14,16},{16,18},{18... | collective-permute-start | bytes 2654216 | tf_op jit(solution)/shard_map/ppermute | solution.py:228
  50.1 1.9 %collective-permute-start.8 = (bf16[96,4608]{1,0:T(8,128)(2,1)S(1)}, bf16[96,4608]{1,0:T(8,128)(2,1)S(1)}, u32[]{:S(2)}, u32[]{:S(2)}) collective-permute-start(bf16[96,4608]{1,0:T(8,128)(2,1)S(1)} %get-tuple-element.34), channel_id=1, source_target_pairs={{2,0},{4,2},{6,4},{8,6},{10,8},{12,10},{14,12},{16,14},{18,16},{20... | collective-permute-start | bytes 2654216 | tf_op jit(solution)/shard_map/ppermute | solution.py:228
  52.0 8.1 %products.5 = s32[80,2688]{1,0:T(8,128)S(1)} custom-call(s32[360]{0:T(512)S(1)} %reshape.8.index_ref, bf16[80,4608]{1,0:T(8,128)(2,1)S(1)} %collective-permute-done.2.refs_0_, bf16[80,5120]{1,0:T(8,128)(2,1)S(1)} %collective-permute-done.1.refs_1_, bf16[80,4608]{1,0:T(8,128)(2,1)S(1)} %collective-permute-done.3.refs_2_, bf16[40,9,128,128]{3,2,1,0:T(8,128)(2,1)} %refs_3_.9), custom_call_target="tpu_custom_call" | custom-call | flops 1 | bytes 1 | tf_op jit(solution)/shard_map/products/pallas_call | solution.py:133
  61.4 7.8 %products.6.own_ref = f32[112,5120]{1,0:T(8,128)S(1)} custom-call(s32[360]{0:T(512)S(1)} %reshape.8.index_ref, bf16[112,4608]{1,0:T(8,128)(2,1)} %collective-permute-done.4.refs_0_, bf16[256,5120]{1,0:T(8,128)(2,1)S(1)} %copy-done, bf16[112,4608]{1,0:T(8,128)(2,1)} %collective-permute-done.5.refs_2_, bf16[40,9,128,128]{3,2,1,0:T(8,128)(2,1)} %refs_3_.9), custom_call_target="tpu_custom_call" | custom-call | flops 1 | bytes 1 | tf_op jit(solution)/shard_map/products/pallas_call | solution.py:133
  69.3 3.9 %collective-permute-start.13 = (bf16[80,4608]{1,0:T(8,128)(2,1)S(1)}, bf16[80,4608]{1,0:T(8,128)(2,1)S(1)}, u32[]{:S(2)}, u32[]{:S(2)}) collective-permute-start(bf16[80,4608]{1,0:T(8,128)(2,1)S(1)} %get-tuple-element.21), channel_id=1, source_target_pairs={{0,2},{2,4},{4,6},{6,8},{8,10},{10,12},{12,14},{14,16},{16,18},{18... | collective-permute-start | bytes 2211848 | tf_op jit(solution)/shard_map/ppermute | solution.py:228
  73.2 1.9 %collective-permute-start.14 = (bf16[80,4608]{1,0:T(8,128)(2,1)S(1)}, bf16[80,4608]{1,0:T(8,128)(2,1)S(1)}, u32[]{:S(2)}, u32[]{:S(2)}) collective-permute-start(bf16[80,4608]{1,0:T(8,128)(2,1)S(1)} %get-tuple-element.22), channel_id=1, source_target_pairs={{2,0},{4,2},{6,4},{8,6},{10,8},{12,10},{14,12},{16,14},{18,16},{20... | collective-permute-start | bytes 2211848 | tf_op jit(solution)/shard_map/ppermute | solution.py:228
  75.2 8.4 %products.7 = s32[96,2688]{1,0:T(8,128)S(1)} custom-call(s32[360]{0:T(512)S(1)} %reshape.8.index_ref, bf16[96,4608]{1,0:T(8,128)(2,1)S(1)} %collective-permute-done.7.refs_0_, bf16[96,5120]{1,0:T(8,128)(2,1)} %collective-permute-done.refs_1_, bf16[96,4608]{1,0:T(8,128)(2,1)S(1)} %collective-permute-done.8.refs_2_, bf16[40,9,128,128]{3,2,1,0:T(8,128)(2,1)} %refs_3_.9), custom_call_target="tpu_custom_call" | custom-call | flops 1 | bytes 1 | tf_op jit(solution)/shard_map/products/pallas_call | solution.py:133
  84.1 1.6 %finish.4.refs_2_ = bf16[256,5120]{1,0:T(8,128)(2,1)} custom-call(f32[112,5120]{1,0:T(8,128)S(1)} %products.6.own_ref, s32[80,2688]{1,0:T(8,128)S(1)} %collective-permute-done.9.refs_0_.refs_1_, s32[80,2688]{1,0:T(8,128)S(1)} %collective-permute-done.9.refs_0_.refs_1_), custom_call_target="tpu_custom_call" | custom-call | flops 1 | bytes 1 | tf_op jit(solution)/shard_map/finish/pallas_call | solution.py:186
  85.7 3.9 %collective-permute-start.11 = (bf16[144,4608]{1,0:T(8,128)(2,1)S(1)}, bf16[144,4608]{1,0:T(8,128)(2,1)S(1)}, u32[]{:S(2)}, u32[]{:S(2)}) collective-permute-start(bf16[144,4608]{1,0:T(8,128)(2,1)S(1)} %get-tuple-element.26), channel_id=1, source_target_pairs={{0,2},{2,4},{4,6},{6,8},{8,10},{10,12},{12,14},{14,16},{16,18},{18... | collective-permute-start | bytes 3981320 | tf_op jit(solution)/shard_map/ppermute | solution.py:228
  89.6 1.9 %collective-permute-start.12 = (bf16[144,4608]{1,0:T(8,128)(2,1)S(1)}, bf16[144,4608]{1,0:T(8,128)(2,1)S(1)}, u32[]{:S(2)}, u32[]{:S(2)}) collective-permute-start(bf16[144,4608]{1,0:T(8,128)(2,1)S(1)} %get-tuple-element.27), channel_id=1, source_target_pairs={{2,0},{4,2},{6,4},{8,6},{10,8},{12,10},{14,12},{16,14},{18,16},{20... | collective-permute-start | bytes 3981320 | tf_op jit(solution)/shard_map/ppermute | solution.py:228
  91.6 8.1 %products.9 = s32[80,2688]{1,0:T(8,128)S(1)} custom-call(s32[360]{0:T(512)S(1)} %reshape.8.index_ref, bf16[80,4608]{1,0:T(8,128)(2,1)S(1)} %collective-permute-done.13.refs_0_, bf16[80,5120]{1,0:T(8,128)(2,1)S(1)} %collective-permute-done.6.refs_1_, bf16[80,4608]{1,0:T(8,128)(2,1)S(1)} %collective-permute-done.14.refs_2_, bf16[40,9,128,128]{3,2,1,0:T(8,128)(2,1)} %refs_3_.9), custom_call_target="tpu_custom_call" | custom-call | flops 1 | bytes 1 | tf_op jit(solution)/shard_map/products/pallas_call | solution.py:133
  99.7 7.1 %collective-permute-done.10.refs_0_.refs_1_ = s32[96,2688]{1,0:T(8,128)S(1)} collective-permute-done((s32[96,2688]{1,0:T(8,128)S(1)}, s32[96,2688]{1,0:T(8,128)S(1)}, u32[]{:S(2)}, u32[]{:S(2)}) %collective-permute-start.10) | collective-permute-done | bytes 1032224 | tf_op jit(solution)/shard_map/ppermute | solution.py:231
  108.1 10.4 %collective-permute-done.11.refs_0_ = bf16[144,4608]{1,0:T(8,128)(2,1)S(1)} collective-permute-done((bf16[144,4608]{1,0:T(8,128)(2,1)S(1)}, bf16[144,4608]{1,0:T(8,128)(2,1)S(1)}, u32[]{:S(2)}, u32[]{:S(2)}) %collective-permute-start.11) | collective-permute-done | bytes 1327136 | tf_op jit(solution)/shard_map/ppermute | solution.py:228
  118.5 2.5 %collective-permute-done.12.refs_2_ = bf16[144,4608]{1,0:T(8,128)(2,1)S(1)} collective-permute-done((bf16[144,4608]{1,0:T(8,128)(2,1)S(1)}, bf16[144,4608]{1,0:T(8,128)(2,1)S(1)}, u32[]{:S(2)}, u32[]{:S(2)}) %collective-permute-start.12) | collective-permute-done | bytes 1327136 | tf_op jit(solution)/shard_map/ppermute | solution.py:228
  121.0 7.2 %products.8.own_ref = f32[144,5120]{1,0:T(8,128)S(1)} custom-call(s32[360]{0:T(512)S(1)} %reshape.8.index_ref, bf16[144,4608]{1,0:T(8,128)(2,1)S(1)} %collective-permute-done.11.refs_0_, bf16[256,5120]{1,0:T(8,128)(2,1)S(1)} %copy-done, bf16[144,4608]{1,0:T(8,128)(2,1)S(1)} %collective-permute-done.12.refs_2_, bf16[40,9,128,128]{3,2,1,0:T(8,128)(2,1)} %refs_3_.9), custom_call_target="tpu_custom_call" | custom-call | flops 1 | bytes 1 | tf_op jit(solution)/shard_map/products/pallas_call | solution.py:133
  (35 shorter events, 11.1 us)
Async XLA Ops:
  0.0 12.4 %copy-start = (bf16[256,5120]{1,0:T(8,128)(2,1)S(1)}, bf16[256,5120]{1,0:T(8,128)(2,1)}, u32[]{:S(2)}) copy-start(bf16[256,5120]{1,0:T(8,128)(2,1)} %refs_1_.3) | copy-start | bytes 7864324
  2.3 11.4 %copy-start.1 = (s32[40,9]{0,1:T(8,128)S(1)}, s32[40,9]{0,1:T(8,128)}, u32[]{:S(2)}) copy-start(s32[40,9]{0,1:T(8,128)} %param.6) | copy-start | bytes 4324
  2.3 11.4 %copy-start.2 = (s32[40]{0:T(128)S(1)}, s32[40]{0:T(128)}, u32[]{:S(2)}) copy-start(s32[40]{0:T(128)} %param.7) | copy-start | bytes 484
  2.3 19.4 %collective-permute-start.1 = (bf16[80,5120]{1,0:T(8,128)(2,1)}, bf16[80,5120]{1,0:T(8,128)(2,1)S(1)}, u32[]{:S(2)}, u32[]{:S(2)}) collective-permute-start(bf16[80,5120]{1,0:T(8,128)(2,1)} %slice.50), channel_id=1, source_target_pairs={{0,1},{1,0},{2,3},{3,2},{4,5},{5,4},{6,7},{7,6},{8,9},{9,8},{10,11... | collective-permute-start | bytes 2457608 | tf_op jit(solution)/shard_map/ppermute | solution.py:231
  6.5 34.8 %collective-permute-start.4 = (bf16[112,4608]{1,0:T(8,128)(2,1)}, bf16[112,4608]{1,0:T(8,128)(2,1)}, u32[]{:S(2)}, u32[]{:S(2)}) collective-permute-start(bf16[112,4608]{1,0:T(8,128)(2,1)} %get-tuple-element.31), channel_id=1, source_target_pairs={{0,2},{2,4},{4,6},{6,8},{8,10},{10,12},{12,14},{14,16},{16,18},{18... | collective-permute-start | bytes 3096584 | tf_op jit(solution)/shard_map/ppermute | solution.py:228
  10.5 32.7 %collective-permute-start.5 = (bf16[112,4608]{1,0:T(8,128)(2,1)}, bf16[112,4608]{1,0:T(8,128)(2,1)}, u32[]{:S(2)}, u32[]{:S(2)}) collective-permute-start(bf16[112,4608]{1,0:T(8,128)(2,1)} %get-tuple-element.32), channel_id=1, source_target_pairs={{2,0},{4,2},{6,4},{8,6},{10,8},{12,10},{14,12},{16,14},{18,16},{20... | collective-permute-start | bytes 3096584 | tf_op jit(solution)/shard_map/ppermute | solution.py:228
  13.4 30.1 %collective-permute-start = (bf16[96,5120]{1,0:T(8,128)(2,1)}, bf16[96,5120]{1,0:T(8,128)(2,1)}, u32[]{:S(2)}, u32[]{:S(2)}) collective-permute-start(bf16[96,5120]{1,0:T(8,128)(2,1)} %slice.47), channel_id=1, source_target_pairs={{0,1},{1,0},{2,3},{3,2},{4,5},{5,4},{6,7},{7,6},{8,9},{9,8},{10,11... | collective-permute-start | bytes 2949128 | tf_op jit(solution)/shard_map/ppermute | solution.py:231
  21.8 30.2 %collective-permute-start.2 = (bf16[80,4608]{1,0:T(8,128)(2,1)S(1)}, bf16[80,4608]{1,0:T(8,128)(2,1)S(1)}, u32[]{:S(2)}, u32[]{:S(2)}) collective-permute-start(bf16[80,4608]{1,0:T(8,128)(2,1)S(1)} %get-tuple-element.37), channel_id=1, source_target_pairs={{0,2},{2,4},{4,6},{6,8},{8,10},{10,12},{12,14},{14,16},{16,18},{18... | collective-permute-start | bytes 2211848 | tf_op jit(solution)/shard_map/ppermute | solution.py:228
  27.5 24.6 %collective-permute-start.3 = (bf16[80,4608]{1,0:T(8,128)(2,1)S(1)}, bf16[80,4608]{1,0:T(8,128)(2,1)S(1)}, u32[]{:S(2)}, u32[]{:S(2)}) collective-permute-start(bf16[80,4608]{1,0:T(8,128)(2,1)S(1)} %get-tuple-element.38), channel_id=1, source_target_pairs={{2,0},{4,2},{6,4},{8,6},{10,8},{12,10},{14,12},{16,14},{18,16},{20... | collective-permute-start | bytes 2211848 | tf_op jit(solution)/shard_map/ppermute | solution.py:228
  43.2 26.0 %collective-permute-start.6 = (bf16[80,5120]{1,0:T(8,128)(2,1)S(1)}, bf16[80,5120]{1,0:T(8,128)(2,1)S(1)}, u32[]{:S(2)}, u32[]{:S(2)}) collective-permute-start(bf16[80,5120]{1,0:T(8,128)(2,1)S(1)} %slice.53), channel_id=1, source_target_pairs={{0,1},{1,0},{2,3},{3,2},{4,5},{5,4},{6,7},{7,6},{8,9},{9,8},{10,11... | collective-permute-start | bytes 2457608 | tf_op jit(solution)/shard_map/ppermute | solution.py:231
  45.1 30.1 %collective-permute-start.7 = (bf16[96,4608]{1,0:T(8,128)(2,1)S(1)}, bf16[96,4608]{1,0:T(8,128)(2,1)S(1)}, u32[]{:S(2)}, u32[]{:S(2)}) collective-permute-start(bf16[96,4608]{1,0:T(8,128)(2,1)S(1)} %get-tuple-element.33), channel_id=1, source_target_pairs={{0,2},{2,4},{4,6},{6,8},{8,10},{10,12},{12,14},{14,16},{16,18},{18... | collective-permute-start | bytes 2654216 | tf_op jit(solution)/shard_map/ppermute | solution.py:228
  50.1 25.1 %collective-permute-start.8 = (bf16[96,4608]{1,0:T(8,128)(2,1)S(1)}, bf16[96,4608]{1,0:T(8,128)(2,1)S(1)}, u32[]{:S(2)}, u32[]{:S(2)}) collective-permute-start(bf16[96,4608]{1,0:T(8,128)(2,1)S(1)} %get-tuple-element.34), channel_id=1, source_target_pairs={{2,0},{4,2},{6,4},{8,6},{10,8},{12,10},{14,12},{16,14},{18,16},{20... | collective-permute-start | bytes 2654216 | tf_op jit(solution)/shard_map/ppermute | solution.py:228
  60.1 23.5 %collective-permute-start.9 = (s32[80,2688]{1,0:T(8,128)S(1)}, s32[80,2688]{1,0:T(8,128)S(1)}, u32[]{:S(2)}, u32[]{:S(2)}) collective-permute-start(s32[80,2688]{1,0:T(8,128)S(1)} %products.5), channel_id=1, source_target_pairs={{0,1},{1,0},{2,3},{3,2},{4,5},{5,4},{6,7},{7,6},{8,9},{9,8},{10,11... | collective-permute-start | bytes 2580488 | tf_op jit(solution)/shard_map/ppermute | solution.py:231
  69.3 22.2 %collective-permute-start.13 = (bf16[80,4608]{1,0:T(8,128)(2,1)S(1)}, bf16[80,4608]{1,0:T(8,128)(2,1)S(1)}, u32[]{:S(2)}, u32[]{:S(2)}) collective-permute-start(bf16[80,4608]{1,0:T(8,128)(2,1)S(1)} %get-tuple-element.21), channel_id=1, source_target_pairs={{0,2},{2,4},{4,6},{6,8},{8,10},{10,12},{12,14},{14,16},{16,18},{18... | collective-permute-start | bytes 2211848 | tf_op jit(solution)/shard_map/ppermute | solution.py:228
  73.2 18.3 %collective-permute-start.14 = (bf16[80,4608]{1,0:T(8,128)(2,1)S(1)}, bf16[80,4608]{1,0:T(8,128)(2,1)S(1)}, u32[]{:S(2)}, u32[]{:S(2)}) collective-permute-start(bf16[80,4608]{1,0:T(8,128)(2,1)S(1)} %get-tuple-element.22), channel_id=1, source_target_pairs={{2,0},{4,2},{6,4},{8,6},{10,8},{12,10},{14,12},{16,14},{18,16},{20... | collective-permute-start | bytes 2211848 | tf_op jit(solution)/shard_map/ppermute | solution.py:228
  83.6 23.1 %collective-permute-start.10 = (s32[96,2688]{1,0:T(8,128)S(1)}, s32[96,2688]{1,0:T(8,128)S(1)}, u32[]{:S(2)}, u32[]{:S(2)}) collective-permute-start(s32[96,2688]{1,0:T(8,128)S(1)} %products.7), channel_id=1, source_target_pairs={{0,1},{1,0},{2,3},{3,2},{4,5},{5,4},{6,7},{7,6},{8,9},{9,8},{10,11... | collective-permute-start | bytes 3096584 | tf_op jit(solution)/shard_map/ppermute | solution.py:231
  85.7 32.8 %collective-permute-start.11 = (bf16[144,4608]{1,0:T(8,128)(2,1)S(1)}, bf16[144,4608]{1,0:T(8,128)(2,1)S(1)}, u32[]{:S(2)}, u32[]{:S(2)}) collective-permute-start(bf16[144,4608]{1,0:T(8,128)(2,1)S(1)} %get-tuple-element.26), channel_id=1, source_target_pairs={{0,2},{2,4},{4,6},{6,8},{8,10},{10,12},{12,14},{14,16},{16,18},{18... | collective-permute-start | bytes 3981320 | tf_op jit(solution)/shard_map/ppermute | solution.py:228
  89.6 31.4 %collective-permute-start.12 = (bf16[144,4608]{1,0:T(8,128)(2,1)S(1)}, bf16[144,4608]{1,0:T(8,128)(2,1)S(1)}, u32[]{:S(2)}, u32[]{:S(2)}) collective-permute-start(bf16[144,4608]{1,0:T(8,128)(2,1)S(1)} %get-tuple-element.27), channel_id=1, source_target_pairs={{2,0},{4,2},{6,4},{8,6},{10,8},{12,10},{14,12},{16,14},{18,16},{20... | collective-permute-start | bytes 3981320 | tf_op jit(solution)/shard_map/ppermute | solution.py:228
  106.7 23.0 %collective-permute-start.15 = (s32[80,2688]{1,0:T(8,128)S(1)}, s32[80,2688]{1,0:T(8,128)S(1)}, u32[]{:S(2)}, u32[]{:S(2)}) collective-permute-start(s32[80,2688]{1,0:T(8,128)S(1)} %products.9), channel_id=1, source_target_pairs={{0,1},{1,0},{2,3},{3,2},{4,5},{5,4},{6,7},{7,6},{8,9},{9,8},{10,11... | collective-permute-start | bytes 2580488 | tf_op jit(solution)/shard_map/ppermute | solution.py:231
where the time goes:
time: 132 us; the launch traced here: 131 us
  Pallas kernels  45.4 us (34%)
  waiting for transfers between devices  41.5 us (31%)
  starting transfers between devices  35.6 us (27%)
  local copies, waits for them, and re-layouts  8.48 us (6%)
    pallas_call x5, Pallas kernels, products(): pl.pallas_call(functools.partial(products_kernel, plan, group, slots, blo...  39.6 us
    ppermute x5, starting transfers between devices, halo(): lax.ppermute(edges[0], 'basis', up)  22.4 us
    ppermute x5, waiting for transfers between devices, halo(): lax.ppermute(edges[0], 'basis', up)  22.4 us
    ppermute x6, waiting for transfers between devices, shifted(): lax.ppermute(piece, 'state', [(i, (i + shift) % state_size) for i in rang...  14.8 us
    ppermute x5, starting transfers between devices, halo(): lax.ppermute(edges[1], 'basis', down)  9.6 us
    pallas_call x4, Pallas kernels, finish(): pl.pallas_call(functools.partial(finish_kernel, len(coded), block, pairs)...  5.77 us
    slice x5, local copies, waits for them, and re-layouts, edges_of(): edges = (piece[:, width - reach:], piece[:, :reach])  4.91 us
    ppermute x5, waiting for transfers between devices, halo(): lax.ppermute(edges[1], 'basis', down)  4.37 us
  transfers between devices with their start and end apart: 16, of which 6 were waited for; matrix products, arithmetic and copies ran while one was open for 5% of the time, Pallas kernels for 33%

commit v1 on v0

--- a/solution.py
+++ b/solution.py
@@ -148,43 +148,56 @@
     )(index, *sources, pltpu.with_memory_space_constraint(blocks, pltpu.HBM))
 
 
-def finish_kernel(partials, block, pairs, own_ref, *refs):
+def finish_kernel(pieces, block, pairs, own_ref, *refs):
     out_ref = refs[-1]
     step = pl.program_id(0)
-    lane = lax.broadcasted_iota(jnp.int32, (own_ref.shape[0], block), 1)
-    levels = [level_of(refs[2 * p + 1][...]) * (1.0 / TOP) for p in range(partials)]
-    for pair in range(pairs):
-        for half in range(2):
-            at = (2 * pair + half) * block
-            row = (step * pairs + pair) * 2 + half
-            total = own_ref[:, at : at + block]
-            for p in range(partials):
-                word = refs[2 * p][:, pair * block : (pair + 1) * block]
-                value = (word >> 16) if half else ((word << 16) >> 16)
-                level = jnp.max(jnp.where(lane == row, levels[p], 0.0), axis=1, keepdims=True)
-                total = total + value.astype(jnp.float32) * level
-            out_ref[:, at : at + block] = total.astype(out_ref.dtype)
-
-
-def finish(own_sums, own_start, coded, coded_start, out, start, size, states, block):
+    n = 0
+    for offset, length, partials in pieces:
+        lane = lax.broadcasted_iota(jnp.int32, (length, block), 1)
+        rows = pl.ds(offset, length)
+        some = [refs[2 * p : 2 * p + 2] for p in range(n, n + partials)]
+        levels = [level_of(codes[...]) * (1.0 / TOP) for _, codes in some]
+        n += partials
+        for pair in range(pairs):
+            for half in range(2):
+                at = (2 * pair + half) * block
+                row = (step * pairs + pair) * 2 + half
+                total = own_ref[rows, at : at + block]
+                for (words, _), mine in zip(some, levels):
+                    word = words[:, pair * block : (pair + 1) * block]
+                    value = (word >> 16) if half else ((word << 16) >> 16)
+                    level = jnp.max(jnp.where(lane == row, mine, 0.0), axis=1, keepdims=True)
+                    total = total + value.astype(jnp.float32) * level
+                out_ref[rows, at : at + block] = total.astype(out_ref.dtype)
+
+
+def finish(own_sums, own_start, pieces, out, states, block):
     width = own_sums.shape[1]
     words = width // block // 2
     pairs = words // 2 if words % 2 == 0 else 1
-    rows, wide, narrow = pl.Element(size), pl.Element(2 * pairs * block), pl.Element(pairs * block)
-    own_at, coded_at = start - own_start, start - coded_start
+    start, size = pieces[0][0], sum(piece[1] for piece in pieces)
+    rows, wide = pl.Element(size), pl.Element(2 * pairs * block)
+    own_at = start - own_start
     in_specs = [pl.BlockSpec((rows, wide), lambda i: (own_at, i * 2 * pairs * block))]
-    operands = [own_sums]
-    for array in coded:
-        in_specs.append(pl.BlockSpec((rows, narrow), lambda i: (coded_at, i * pairs * block)))
-        in_specs.append(pl.BlockSpec((rows, pl.Element(block)), lambda i: (coded_at, words * block)))
-        operands += [array, array]
+    operands, shapes = [own_sums], []
+    for at, length, arrays, coded_start in pieces:
+        shapes.append((at - start, length, len(arrays)))
+        some, first = pl.Element(length), at - coded_start
+        for array in arrays:
+            in_specs.append(
+                pl.BlockSpec((some, pl.Element(pairs * block)), lambda i, first=first: (first, i * pairs * block))
+            )
+            in_specs.append(
+                pl.BlockSpec((some, pl.Element(block)), lambda i, first=first: (first, words * block))
+            )
+            operands += [array, array]
     aliases = {}
     if out is not None:
         aliases = {len(operands): 0}
         in_specs.append(pl.BlockSpec(memory_space=pl.ANY))
         operands.append(out)
     return pl.pallas_call(
-        functools.partial(finish_kernel, len(coded), block, pairs),
+        functools.partial(finish_kernel, tuple(shapes), block, pairs),
         out_shape=jax.ShapeDtypeStruct((states, width), jnp.bfloat16),
         grid=(words // pairs,),
         in_specs=in_specs,
@@ -267,20 +280,20 @@
         received.append(shifted(message, -shift))
         coded[c].append(received[n])
 
-    def finish_piece(part, c, out):
-        own_end, end = own_starts[part] + own_sizes[part], starts[c] + sizes[c]
-        at, end = max(own_starts[part], starts[c]), min(own_end, end)
-        if at >= end:
-            return out
-        return finish(
-            own_sums[part], own_starts[part], coded[c], starts[c], out, at, end - at, states, block
-        )
+    def finish_pieces(part, chunks, out):
+        pieces = []
+        for c in chunks:
+            at = max(own_starts[part], starts[c])
+            end = min(own_starts[part] + own_sizes[part], starts[c] + sizes[c])
+            if at < end:
+                pieces.append((at, end - at, coded[c], starts[c]))
+        return finish(own_sums[part], own_starts[part], pieces, out, states, block) if pieces else out
 
     out, done = None, set()
     if len(own_sizes) > 1:
         send(0)
         if state_size == 2:
-            out = finish_piece(0, 0, out)
+            out = finish_pieces(0, (0,), out)
             done.add((0, 0))
         held = (out,) if done else ()
         last = halo(own_edges(1, *edges[-1], *sent[-1:], *held))
@@ -290,9 +303,7 @@
     for part in range(len(own_sizes)):
         if part:
             own_sums += products(after(index, out), [own_part(part, last)], blocks)
-        for c in range(len(sizes)):
-            if (part, c) not in done:
-                out = finish_piece(part, c, out)
+        out = finish_pieces(part, [c for c in range(len(sizes)) if (part, c) not in done], out)
     return out
 
 

time: 132 us -> 131 us (level)
    pallas_call x4 -> x3, Pallas kernels: 5.77 us -> 4.93 us  [finish(): pl.pallas_call(functools.partial(finish_kernel, tuple(shapes), block, pai...]
  transfers between devices with their start and end apart: 16 -> 16, of which waited for: 6 -> 6; matrix products, arithmetic and copies ran while one was open for 5% -> 5% of each run, Pallas kernels for 33% -> 32%
where the time goes in v1:
time: 131 us; the launch traced here: 130 us
  Pallas kernels  44.5 us (34%)
  waiting for transfers between devices  41.2 us (31%)
  starting transfers between devices  35.8 us (27%)
  local copies, waits for them, and re-layouts  8.48 us (6%)
    pallas_call x5, Pallas kernels, products(): pl.pallas_call(functools.partial(products_kernel, plan, group, slots, blo...  39.6 us
    ppermute x5, starting transfers between devices, halo(): lax.ppermute(edges[0], 'basis', up)  22.3 us
    ppermute x5, waiting for transfers between devices, halo(): lax.ppermute(edges[0], 'basis', up)  22.3 us
    ppermute x6, waiting for transfers between devices, shifted(): lax.ppermute(piece, 'state', [(i, (i + shift) % state_size) for i in rang...  14.7 us
    ppermute x5, starting transfers between devices, halo(): lax.ppermute(edges[1], 'basis', down)  9.6 us
    pallas_call x3, Pallas kernels, finish(): pl.pallas_call(functools.partial(finish_kernel, tuple(shapes), block, pai...  4.93 us
    slice x5, local copies, waits for them, and re-layouts, edges_of(): edges = (piece[:, width - reach:], piece[:, :reach])  4.91 us
    ppermute x5, waiting for transfers between devices, halo(): lax.ppermute(edges[1], 'basis', down)  4.28 us
  transfers between devices with their start and end apart: 16, of which 6 were waited for; matrix products, arithmetic and copies ran while one was open for 5% of the time, Pallas kernels for 32%

profile of v1, /device:TPU:9, one launch (start us, length us, event | category | flops | bytes accessed | tf_op | source)
XLA Modules:
  0.0 130.4 jit_solution(17850828693297135962)
XLA Ops:
  0.0 2.3 %slice.50 = bf16[80,5120]{1,0:T(8,128)(2,1)} slice(bf16[256,5120]{1,0:T(8,128)(2,1)} %refs_1_.3), slice={[0:80], [0:5120]} | slice | bytes 1638400 | tf_op jit(solution)/shard_map/slice | solution.py:262
  3.5 3.0 %fusion.1 = (bf16[112,4608]{1,0:T(8,128)(2,1)}, bf16[112,4608]{1,0:T(8,128)(2,1)}) fusion(bf16[256,5120]{1,0:T(8,128)(2,1)} %refs_1_.3), kind=kLoop, calls=%fused_computation.3 | loop fusion | bytes 4128768 | tf_op jit(solution)/shard_map/slice | solution.py:237
  6.5 4.0 %collective-permute-start.4 = (bf16[112,4608]{1,0:T(8,128)(2,1)}, bf16[112,4608]{1,0:T(8,128)(2,1)}, u32[]{:S(2)}, u32[]{:S(2)}) collective-permute-start(bf16[112,4608]{1,0:T(8,128)(2,1)} %get-tuple-element.31), channel_id=1, source_target_pairs={{0,2},{2,4},{4,6},{6,8},{8,10},{10,12},{12,14},{14,16},{16,18},{18... | collective-permute-start | bytes 3096584 | tf_op jit(solution)/shard_map/ppermute | solution.py:241
  10.5 1.9 %collective-permute-start.5 = (bf16[112,4608]{1,0:T(8,128)(2,1)}, bf16[112,4608]{1,0:T(8,128)(2,1)}, u32[]{:S(2)}, u32[]{:S(2)}) collective-permute-start(bf16[112,4608]{1,0:T(8,128)(2,1)} %get-tuple-element.32), channel_id=1, source_target_pairs={{2,0},{4,2},{6,4},{8,6},{10,8},{12,10},{14,12},{16,14},{18,16},{20... | collective-permute-start | bytes 3096584 | tf_op jit(solution)/shard_map/ppermute | solution.py:241
  14.0 7.7 %collective-permute-done.1.refs_1_ = bf16[80,5120]{1,0:T(8,128)(2,1)S(1)} collective-permute-done((bf16[80,5120]{1,0:T(8,128)(2,1)}, bf16[80,5120]{1,0:T(8,128)(2,1)S(1)}, u32[]{:S(2)}, u32[]{:S(2)}) %collective-permute-start.1) | collective-permute-done | bytes 819232 | tf_op jit(solution)/shard_map/ppermute | solution.py:244
  21.8 5.6 %collective-permute-start.2 = (bf16[80,4608]{1,0:T(8,128)(2,1)S(1)}, bf16[80,4608]{1,0:T(8,128)(2,1)S(1)}, u32[]{:S(2)}, u32[]{:S(2)}) collective-permute-start(bf16[80,4608]{1,0:T(8,128)(2,1)S(1)} %get-tuple-element.37), channel_id=1, source_target_pairs={{0,2},{2,4},{4,6},{6,8},{8,10},{10,12},{12,14},{14,16},{16,18},{18... | collective-permute-start | bytes 2211848 | tf_op jit(solution)/shard_map/ppermute | solution.py:241
  27.5 1.9 %collective-permute-start.3 = (bf16[80,4608]{1,0:T(8,128)(2,1)S(1)}, bf16[80,4608]{1,0:T(8,128)(2,1)S(1)}, u32[]{:S(2)}, u32[]{:S(2)}) collective-permute-start(bf16[80,4608]{1,0:T(8,128)(2,1)S(1)} %get-tuple-element.38), channel_id=1, source_target_pairs={{2,0},{4,2},{6,4},{8,6},{10,8},{12,10},{14,12},{16,14},{18,16},{20... | collective-permute-start | bytes 2211848 | tf_op jit(solution)/shard_map/ppermute | solution.py:241
  29.4 11.9 %collective-permute-done.4.refs_0_ = bf16[112,4608]{1,0:T(8,128)(2,1)} collective-permute-done((bf16[112,4608]{1,0:T(8,128)(2,1)}, bf16[112,4608]{1,0:T(8,128)(2,1)}, u32[]{:S(2)}, u32[]{:S(2)}) %collective-permute-start.4) | collective-permute-done | bytes 1032224 | tf_op jit(solution)/shard_map/ppermute | solution.py:241
  41.3 1.9 %collective-permute-done.5.refs_2_ = bf16[112,4608]{1,0:T(8,128)(2,1)} collective-permute-done((bf16[112,4608]{1,0:T(8,128)(2,1)}, bf16[112,4608]{1,0:T(8,128)(2,1)}, u32[]{:S(2)}, u32[]{:S(2)}) %collective-permute-start.5) | collective-permute-done | bytes 1032224 | tf_op jit(solution)/shard_map/ppermute | solution.py:241
  45.1 5.0 %collective-permute-start.7 = (bf16[96,4608]{1,0:T(8,128)(2,1)S(1)}, bf16[96,4608]{1,0:T(8,128)(2,1)S(1)}, u32[]{:S(2)}, u32[]{:S(2)}) collective-permute-start(bf16[96,4608]{1,0:T(8,128)(2,1)S(1)} %get-tuple-element.33), channel_id=1, source_target_pairs={{0,2},{2,4},{4,6},{6,8},{8,10},{10,12},{12,14},{14,16},{16,18},{18... | collective-permute-start | bytes 2654216 | tf_op jit(solution)/shard_map/ppermute | solution.py:241
  50.1 1.9 %collective-permute-start.8 = (bf16[96,4608]{1,0:T(8,128)(2,1)S(1)}, bf16[96,4608]{1,0:T(8,128)(2,1)S(1)}, u32[]{:S(2)}, u32[]{:S(2)}) collective-permute-start(bf16[96,4608]{1,0:T(8,128)(2,1)S(1)} %get-tuple-element.34), channel_id=1, source_target_pairs={{2,0},{4,2},{6,4},{8,6},{10,8},{12,10},{14,12},{16,14},{18,16},{20... | collective-permute-start | bytes 2654216 | tf_op jit(solution)/shard_map/ppermute | solution.py:241
  52.0 8.1 %products.5 = s32[80,2688]{1,0:T(8,128)S(1)} custom-call(s32[360]{0:T(512)S(1)} %reshape.8.index_ref, bf16[80,4608]{1,0:T(8,128)(2,1)S(1)} %collective-permute-done.2.refs_0_, bf16[80,5120]{1,0:T(8,128)(2,1)S(1)} %collective-permute-done.1.refs_1_, bf16[80,4608]{1,0:T(8,128)(2,1)S(1)} %collective-permute-done.3.refs_2_, bf16[40,9,128,128]{3,2,1,0:T(8,128)(2,1)} %refs_3_.9), custom_call_target="tpu_custom_call" | custom-call | flops 1 | bytes 1 | tf_op jit(solution)/shard_map/products/pallas_call | solution.py:133
  61.4 7.8 %products.6.own_ref = f32[112,5120]{1,0:T(8,128)S(1)} custom-call(s32[360]{0:T(512)S(1)} %reshape.8.index_ref, bf16[112,4608]{1,0:T(8,128)(2,1)} %collective-permute-done.4.refs_0_, bf16[256,5120]{1,0:T(8,128)(2,1)S(1)} %copy-done, bf16[112,4608]{1,0:T(8,128)(2,1)} %collective-permute-done.5.refs_2_, bf16[40,9,128,128]{3,2,1,0:T(8,128)(2,1)} %refs_3_.9), custom_call_target="tpu_custom_call" | custom-call | flops 1 | bytes 1 | tf_op jit(solution)/shard_map/products/pallas_call | solution.py:133
  69.4 3.9 %collective-permute-start.13 = (bf16[80,4608]{1,0:T(8,128)(2,1)S(1)}, bf16[80,4608]{1,0:T(8,128)(2,1)S(1)}, u32[]{:S(2)}, u32[]{:S(2)}) collective-permute-start(bf16[80,4608]{1,0:T(8,128)(2,1)S(1)} %get-tuple-element.21), channel_id=1, source_target_pairs={{0,2},{2,4},{4,6},{6,8},{8,10},{10,12},{12,14},{14,16},{16,18},{18... | collective-permute-start | bytes 2211848 | tf_op jit(solution)/shard_map/ppermute | solution.py:241
  73.2 1.9 %collective-permute-start.14 = (bf16[80,4608]{1,0:T(8,128)(2,1)S(1)}, bf16[80,4608]{1,0:T(8,128)(2,1)S(1)}, u32[]{:S(2)}, u32[]{:S(2)}) collective-permute-start(bf16[80,4608]{1,0:T(8,128)(2,1)S(1)} %get-tuple-element.22), channel_id=1, source_target_pairs={{2,0},{4,2},{6,4},{8,6},{10,8},{12,10},{14,12},{16,14},{18,16},{20... | collective-permute-start | bytes 2211848 | tf_op jit(solution)/shard_map/ppermute | solution.py:241
  75.2 8.4 %products.7 = s32[96,2688]{1,0:T(8,128)S(1)} custom-call(s32[360]{0:T(512)S(1)} %reshape.8.index_ref, bf16[96,4608]{1,0:T(8,128)(2,1)S(1)} %collective-permute-done.7.refs_0_, bf16[96,5120]{1,0:T(8,128)(2,1)} %collective-permute-done.refs_1_, bf16[96,4608]{1,0:T(8,128)(2,1)S(1)} %collective-permute-done.8.refs_2_, bf16[40,9,128,128]{3,2,1,0:T(8,128)(2,1)} %refs_3_.9), custom_call_target="tpu_custom_call" | custom-call | flops 1 | bytes 1 | tf_op jit(solution)/shard_map/products/pallas_call | solution.py:133
  85.7 3.9 %collective-permute-start.11 = (bf16[144,4608]{1,0:T(8,128)(2,1)S(1)}, bf16[144,4608]{1,0:T(8,128)(2,1)S(1)}, u32[]{:S(2)}, u32[]{:S(2)}) collective-permute-start(bf16[144,4608]{1,0:T(8,128)(2,1)S(1)} %get-tuple-element.26), channel_id=1, source_target_pairs={{0,2},{2,4},{4,6},{6,8},{8,10},{10,12},{12,14},{14,16},{16,18},{18... | collective-permute-start | bytes 3981320 | tf_op jit(solution)/shard_map/ppermute | solution.py:241
  89.7 1.9 %collective-permute-start.12 = (bf16[144,4608]{1,0:T(8,128)(2,1)S(1)}, bf16[144,4608]{1,0:T(8,128)(2,1)S(1)}, u32[]{:S(2)}, u32[]{:S(2)}) collective-permute-start(bf16[144,4608]{1,0:T(8,128)(2,1)S(1)} %get-tuple-element.27), channel_id=1, source_target_pairs={{2,0},{4,2},{6,4},{8,6},{10,8},{12,10},{14,12},{16,14},{18,16},{20... | collective-permute-start | bytes 3981320 | tf_op jit(solution)/shard_map/ppermute | solution.py:241
  91.6 8.1 %products.9 = s32[80,2688]{1,0:T(8,128)S(1)} custom-call(s32[360]{0:T(512)S(1)} %reshape.8.index_ref, bf16[80,4608]{1,0:T(8,128)(2,1)S(1)} %collective-permute-done.13.refs_0_, bf16[80,5120]{1,0:T(8,128)(2,1)S(1)} %collective-permute-done.6.refs_1_, bf16[80,4608]{1,0:T(8,128)(2,1)S(1)} %collective-permute-done.14.refs_2_, bf16[40,9,128,128]{3,2,1,0:T(8,128)(2,1)} %refs_3_.9), custom_call_target="tpu_custom_call" | custom-call | flops 1 | bytes 1 | tf_op jit(solution)/shard_map/products/pallas_call | solution.py:133
  99.7 6.9 %collective-permute-done.10.refs_0_.refs_1_ = s32[96,2688]{1,0:T(8,128)S(1)} collective-permute-done((s32[96,2688]{1,0:T(8,128)S(1)}, s32[96,2688]{1,0:T(8,128)S(1)}, u32[]{:S(2)}, u32[]{:S(2)}) %collective-permute-start.10) | collective-permute-done | bytes 1032224 | tf_op jit(solution)/shard_map/ppermute | solution.py:244
  108.2 10.4 %collective-permute-done.11.refs_0_ = bf16[144,4608]{1,0:T(8,128)(2,1)S(1)} collective-permute-done((bf16[144,4608]{1,0:T(8,128)(2,1)S(1)}, bf16[144,4608]{1,0:T(8,128)(2,1)S(1)}, u32[]{:S(2)}, u32[]{:S(2)}) %collective-permute-start.11) | collective-permute-done | bytes 1327136 | tf_op jit(solution)/shard_map/ppermute | solution.py:241
  118.6 2.4 %collective-permute-done.12.refs_2_ = bf16[144,4608]{1,0:T(8,128)(2,1)S(1)} collective-permute-done((bf16[144,4608]{1,0:T(8,128)(2,1)S(1)}, bf16[144,4608]{1,0:T(8,128)(2,1)S(1)}, u32[]{:S(2)}, u32[]{:S(2)}) %collective-permute-start.12) | collective-permute-done | bytes 1327136 | tf_op jit(solution)/shard_map/ppermute | solution.py:241
  121.0 7.2 %products.8.own_ref = f32[144,5120]{1,0:T(8,128)S(1)} custom-call(s32[360]{0:T(512)S(1)} %reshape.8.index_ref, bf16[144,4608]{1,0:T(8,128)(2,1)S(1)} %collective-permute-done.11.refs_0_, bf16[256,5120]{1,0:T(8,128)(2,1)S(1)} %copy-done, bf16[144,4608]{1,0:T(8,128)(2,1)S(1)} %collective-permute-done.12.refs_2_, bf16[40,9,128,128]{3,2,1,0:T(8,128)(2,1)} %refs_3_.9), custom_call_target="tpu_custom_call" | custom-call | flops 1 | bytes 1 | tf_op jit(solution)/shard_map/products/pallas_call | solution.py:133
  128.2 2.2 %finish.5 = bf16[256,5120]{1,0:T(8,128)(2,1)} custom-call(f32[144,5120]{1,0:T(8,128)S(1)} %products.8.own_ref, s32[96,2688]{1,0:T(8,128)S(1)} %collective-permute-done.10.refs_0_.refs_1_, s32[96,2688]{1,0:T(8,128)S(1)} %collective-permute-done.10.refs_0_.refs_1_, ...), custom_call_target="tpu_custom_call", output_to_operand_aliasing={{}: (5, {})} | custom-call | flops 1 | bytes 1 | tf_op jit(solution)/shard_map/finish/pallas_call | solution.py:199
  (34 shorter events, 9.9 us)
Async XLA Ops:
  0.0 12.4 %copy-start = (bf16[256,5120]{1,0:T(8,128)(2,1)S(1)}, bf16[256,5120]{1,0:T(8,128)(2,1)}, u32[]{:S(2)}) copy-start(bf16[256,5120]{1,0:T(8,128)(2,1)} %refs_1_.3) | copy-start | bytes 7864324
  2.3 11.4 %copy-start.1 = (s32[40,9]{0,1:T(8,128)S(1)}, s32[40,9]{0,1:T(8,128)}, u32[]{:S(2)}) copy-start(s32[40,9]{0,1:T(8,128)} %param.6) | copy-start | bytes 4324
  2.3 11.4 %copy-start.2 = (s32[40]{0:T(128)S(1)}, s32[40]{0:T(128)}, u32[]{:S(2)}) copy-start(s32[40]{0:T(128)} %param.7) | copy-start | bytes 484
  2.3 19.4 %collective-permute-start.1 = (bf16[80,5120]{1,0:T(8,128)(2,1)}, bf16[80,5120]{1,0:T(8,128)(2,1)S(1)}, u32[]{:S(2)}, u32[]{:S(2)}) collective-permute-start(bf16[80,5120]{1,0:T(8,128)(2,1)} %slice.50), channel_id=1, source_target_pairs={{0,1},{1,0},{2,3},{3,2},{4,5},{5,4},{6,7},{7,6},{8,9},{9,8},{10,11... | collective-permute-start | bytes 2457608 | tf_op jit(solution)/shard_map/ppermute | solution.py:244
  6.5 34.8 %collective-permute-start.4 = (bf16[112,4608]{1,0:T(8,128)(2,1)}, bf16[112,4608]{1,0:T(8,128)(2,1)}, u32[]{:S(2)}, u32[]{:S(2)}) collective-permute-start(bf16[112,4608]{1,0:T(8,128)(2,1)} %get-tuple-element.31), channel_id=1, source_target_pairs={{0,2},{2,4},{4,6},{6,8},{8,10},{10,12},{12,14},{14,16},{16,18},{18... | collective-permute-start | bytes 3096584 | tf_op jit(solution)/shard_map/ppermute | solution.py:241
  10.5 32.7 %collective-permute-start.5 = (bf16[112,4608]{1,0:T(8,128)(2,1)}, bf16[112,4608]{1,0:T(8,128)(2,1)}, u32[]{:S(2)}, u32[]{:S(2)}) collective-permute-start(bf16[112,4608]{1,0:T(8,128)(2,1)} %get-tuple-element.32), channel_id=1, source_target_pairs={{2,0},{4,2},{6,4},{8,6},{10,8},{12,10},{14,12},{16,14},{18,16},{20... | collective-permute-start | bytes 3096584 | tf_op jit(solution)/shard_map/ppermute | solution.py:241
  13.4 30.1 %collective-permute-start = (bf16[96,5120]{1,0:T(8,128)(2,1)}, bf16[96,5120]{1,0:T(8,128)(2,1)}, u32[]{:S(2)}, u32[]{:S(2)}) collective-permute-start(bf16[96,5120]{1,0:T(8,128)(2,1)} %slice.47), channel_id=1, source_target_pairs={{0,1},{1,0},{2,3},{3,2},{4,5},{5,4},{6,7},{7,6},{8,9},{9,8},{10,11... | collective-permute-start | bytes 2949128 | tf_op jit(solution)/shard_map/ppermute | solution.py:244
  21.8 30.2 %collective-permute-start.2 = (bf16[80,4608]{1,0:T(8,128)(2,1)S(1)}, bf16[80,4608]{1,0:T(8,128)(2,1)S(1)}, u32[]{:S(2)}, u32[]{:S(2)}) collective-permute-start(bf16[80,4608]{1,0:T(8,128)(2,1)S(1)} %get-tuple-element.37), channel_id=1, source_target_pairs={{0,2},{2,4},{4,6},{6,8},{8,10},{10,12},{12,14},{14,16},{16,18},{18... | collective-permute-start | bytes 2211848 | tf_op jit(solution)/shard_map/ppermute | solution.py:241
  27.5 24.6 %collective-permute-start.3 = (bf16[80,4608]{1,0:T(8,128)(2,1)S(1)}, bf16[80,4608]{1,0:T(8,128)(2,1)S(1)}, u32[]{:S(2)}, u32[]{:S(2)}) collective-permute-start(bf16[80,4608]{1,0:T(8,128)(2,1)S(1)} %get-tuple-element.38), channel_id=1, source_target_pairs={{2,0},{4,2},{6,4},{8,6},{10,8},{12,10},{14,12},{16,14},{18,16},{20... | collective-permute-start | bytes 2211848 | tf_op jit(solution)/shard_map/ppermute | solution.py:241
  43.2 26.0 %collective-permute-start.6 = (bf16[80,5120]{1,0:T(8,128)(2,1)S(1)}, bf16[80,5120]{1,0:T(8,128)(2,1)S(1)}, u32[]{:S(2)}, u32[]{:S(2)}) collective-permute-start(bf16[80,5120]{1,0:T(8,128)(2,1)S(1)} %slice.53), channel_id=1, source_target_pairs={{0,1},{1,0},{2,3},{3,2},{4,5},{5,4},{6,7},{7,6},{8,9},{9,8},{10,11... | collective-permute-start | bytes 2457608 | tf_op jit(solution)/shard_map/ppermute | solution.py:244
  45.1 30.1 %collective-permute-start.7 = (bf16[96,4608]{1,0:T(8,128)(2,1)S(1)}, bf16[96,4608]{1,0:T(8,128)(2,1)S(1)}, u32[]{:S(2)}, u32[]{:S(2)}) collective-permute-start(bf16[96,4608]{1,0:T(8,128)(2,1)S(1)} %get-tuple-element.33), channel_id=1, source_target_pairs={{0,2},{2,4},{4,6},{6,8},{8,10},{10,12},{12,14},{14,16},{16,18},{18... | collective-permute-start | bytes 2654216 | tf_op jit(solution)/shard_map/ppermute | solution.py:241
  50.1 25.1 %collective-permute-start.8 = (bf16[96,4608]{1,0:T(8,128)(2,1)S(1)}, bf16[96,4608]{1,0:T(8,128)(2,1)S(1)}, u32[]{:S(2)}, u32[]{:S(2)}) collective-permute-start(bf16[96,4608]{1,0:T(8,128)(2,1)S(1)} %get-tuple-element.34), channel_id=1, source_target_pairs={{2,0},{4,2},{6,4},{8,6},{10,8},{12,10},{14,12},{16,14},{18,16},{20... | collective-permute-start | bytes 2654216 | tf_op jit(solution)/shard_map/ppermute | solution.py:241
  60.1 23.5 %collective-permute-start.9 = (s32[80,2688]{1,0:T(8,128)S(1)}, s32[80,2688]{1,0:T(8,128)S(1)}, u32[]{:S(2)}, u32[]{:S(2)}) collective-permute-start(s32[80,2688]{1,0:T(8,128)S(1)} %products.5), channel_id=1, source_target_pairs={{0,1},{1,0},{2,3},{3,2},{4,5},{5,4},{6,7},{7,6},{8,9},{9,8},{10,11... | collective-permute-start | bytes 2580488 | tf_op jit(solution)/shard_map/ppermute | solution.py:244
  69.4 22.2 %collective-permute-start.13 = (bf16[80,4608]{1,0:T(8,128)(2,1)S(1)}, bf16[80,4608]{1,0:T(8,128)(2,1)S(1)}, u32[]{:S(2)}, u32[]{:S(2)}) collective-permute-start(bf16[80,4608]{1,0:T(8,128)(2,1)S(1)} %get-tuple-element.21), channel_id=1, source_target_pairs={{0,2},{2,4},{4,6},{6,8},{8,10},{10,12},{12,14},{14,16},{16,18},{18... | collective-permute-start | bytes 2211848 | tf_op jit(solution)/shard_map/ppermute | solution.py:241
  73.2 18.4 %collective-permute-start.14 = (bf16[80,4608]{1,0:T(8,128)(2,1)S(1)}, bf16[80,4608]{1,0:T(8,128)(2,1)S(1)}, u32[]{:S(2)}, u32[]{:S(2)}) collective-permute-start(bf16[80,4608]{1,0:T(8,128)(2,1)S(1)} %get-tuple-element.22), channel_id=1, source_target_pairs={{2,0},{4,2},{6,4},{8,6},{10,8},{12,10},{14,12},{16,14},{18,16},{20... | collective-permute-start | bytes 2211848 | tf_op jit(solution)/shard_map/ppermute | solution.py:241
  83.6 23.1 %collective-permute-start.10 = (s32[96,2688]{1,0:T(8,128)S(1)}, s32[96,2688]{1,0:T(8,128)S(1)}, u32[]{:S(2)}, u32[]{:S(2)}) collective-permute-start(s32[96,2688]{1,0:T(8,128)S(1)} %products.7), channel_id=1, source_target_pairs={{0,1},{1,0},{2,3},{3,2},{4,5},{5,4},{6,7},{7,6},{8,9},{9,8},{10,11... | collective-permute-start | bytes 3096584 | tf_op jit(solution)/shard_map/ppermute | solution.py:244
  85.7 32.8 %collective-permute-start.11 = (bf16[144,4608]{1,0:T(8,128)(2,1)S(1)}, bf16[144,4608]{1,0:T(8,128)(2,1)S(1)}, u32[]{:S(2)}, u32[]{:S(2)}) collective-permute-start(bf16[144,4608]{1,0:T(8,128)(2,1)S(1)} %get-tuple-element.26), channel_id=1, source_target_pairs={{0,2},{2,4},{4,6},{6,8},{8,10},{10,12},{12,14},{14,16},{16,18},{18... | collective-permute-start | bytes 3981320 | tf_op jit(solution)/shard_map/ppermute | solution.py:241
  89.7 31.3 %collective-permute-start.12 = (bf16[144,4608]{1,0:T(8,128)(2,1)S(1)}, bf16[144,4608]{1,0:T(8,128)(2,1)S(1)}, u32[]{:S(2)}, u32[]{:S(2)}) collective-permute-start(bf16[144,4608]{1,0:T(8,128)(2,1)S(1)} %get-tuple-element.27), channel_id=1, source_target_pairs={{2,0},{4,2},{6,4},{8,6},{10,8},{12,10},{14,12},{16,14},{18,16},{20... | collective-permute-start | bytes 3981320 | tf_op jit(solution)/shard_map/ppermute | solution.py:241
  106.6 21.6 %collective-permute-start.15 = (s32[80,2688]{1,0:T(8,128)S(1)}, s32[80,2688]{1,0:T(8,128)S(1)}, u32[]{:S(2)}, u32[]{:S(2)}) collective-permute-start(s32[80,2688]{1,0:T(8,128)S(1)} %products.9), channel_id=1, source_target_pairs={{0,1},{1,0},{2,3},{3,2},{4,5},{5,4},{6,7},{7,6},{8,9},{9,8},{10,11... | collective-permute-start | bytes 2580488 | tf_op jit(solution)/shard_map/ppermute | solution.py:244

commit v2 on v1

--- a/solution.py
+++ b/solution.py
@@ -174,7 +174,8 @@
 def finish(own_sums, own_start, pieces, out, states, block):
     width = own_sums.shape[1]
     words = width // block // 2
-    pairs = words // 2 if words % 2 == 0 else 1
+    steps = 4 if len(pieces) > 1 and words % 4 == 0 else 2
+    pairs = words // steps if words % steps == 0 else 1
     start, size = pieces[0][0], sum(piece[1] for piece in pieces)
     rows, wide = pl.Element(size), pl.Element(2 * pairs * block)
     own_at = start - own_start

time: 131 us -> 131 us (level)
  no operation moved by 1% of the time
where the time goes in v2:
time: 131 us
  Pallas kernels  45 us (34%)
  waiting for transfers between devices  41.7 us (32%)
  starting transfers between devices  35.4 us (27%)
  local copies, waits for them, and re-layouts  8.48 us (6%)
    pallas_call x5, Pallas kernels, products(): pl.pallas_call(functools.partial(products_kernel, plan, group, slots, blo...  39.6 us
    ppermute x5, waiting for transfers between devices, halo(): lax.ppermute(edges[0], 'basis', up)  22.4 us
    ppermute x5, starting transfers between devices, halo(): lax.ppermute(edges[0], 'basis', up)  22.4 us
    ppermute x6, waiting for transfers between devices, shifted(): lax.ppermute(piece, 'state', [(i, (i + shift) % state_size) for i in rang...  14.9 us
    ppermute x5, starting transfers between devices, halo(): lax.ppermute(edges[1], 'basis', down)  9.6 us
    pallas_call x3, Pallas kernels, finish(): pl.pallas_call(functools.partial(finish_kernel, tuple(shapes), block, pai...  5.38 us
    slice x5, local copies, waits for them, and re-layouts, edges_of(): edges = (piece[:, width - reach:], piece[:, :reach])  4.91 us
    ppermute x5, waiting for transfers between devices, halo(): lax.ppermute(edges[1], 'basis', down)  4.44 us
  transfers between devices with their start and end apart: 16, of which 6 were waited for; matrix products, arithmetic and copies ran while one was open for 5% of the time, Pallas kernels for 32%

profile of v2, /device:TPU:9, one launch (start us, length us, event | category | flops | bytes accessed | tf_op | source)
XLA Modules:
  0.0 130.9 jit_solution(875533689724907869)
XLA Ops:
  0.0 2.3 %slice.50 = bf16[80,5120]{1,0:T(8,128)(2,1)} slice(bf16[256,5120]{1,0:T(8,128)(2,1)} %refs_1_.3), slice={[0:80], [0:5120]} | slice | bytes 1638400 | tf_op jit(solution)/shard_map/slice | solution.py:263
  3.5 3.0 %fusion.1 = (bf16[112,4608]{1,0:T(8,128)(2,1)}, bf16[112,4608]{1,0:T(8,128)(2,1)}) fusion(bf16[256,5120]{1,0:T(8,128)(2,1)} %refs_1_.3), kind=kLoop, calls=%fused_computation.3 | loop fusion | bytes 4128768 | tf_op jit(solution)/shard_map/slice | solution.py:238
  6.5 4.0 %collective-permute-start.4 = (bf16[112,4608]{1,0:T(8,128)(2,1)}, bf16[112,4608]{1,0:T(8,128)(2,1)}, u32[]{:S(2)}, u32[]{:S(2)}) collective-permute-start(bf16[112,4608]{1,0:T(8,128)(2,1)} %get-tuple-element.31), channel_id=1, source_target_pairs={{0,2},{2,4},{4,6},{6,8},{8,10},{10,12},{12,14},{14,16},{16,18},{18... | collective-permute-start | bytes 3096584 | tf_op jit(solution)/shard_map/ppermute | solution.py:242
  10.5 1.9 %collective-permute-start.5 = (bf16[112,4608]{1,0:T(8,128)(2,1)}, bf16[112,4608]{1,0:T(8,128)(2,1)}, u32[]{:S(2)}, u32[]{:S(2)}) collective-permute-start(bf16[112,4608]{1,0:T(8,128)(2,1)} %get-tuple-element.32), channel_id=1, source_target_pairs={{2,0},{4,2},{6,4},{8,6},{10,8},{12,10},{14,12},{16,14},{18,16},{20... | collective-permute-start | bytes 3096584 | tf_op jit(solution)/shard_map/ppermute | solution.py:242
  14.0 7.7 %collective-permute-done.1.refs_1_ = bf16[80,5120]{1,0:T(8,128)(2,1)S(1)} collective-permute-done((bf16[80,5120]{1,0:T(8,128)(2,1)}, bf16[80,5120]{1,0:T(8,128)(2,1)S(1)}, u32[]{:S(2)}, u32[]{:S(2)}) %collective-permute-start.1) | collective-permute-done | bytes 819232 | tf_op jit(solution)/shard_map/ppermute | solution.py:245
  21.8 5.6 %collective-permute-start.2 = (bf16[80,4608]{1,0:T(8,128)(2,1)S(1)}, bf16[80,4608]{1,0:T(8,128)(2,1)S(1)}, u32[]{:S(2)}, u32[]{:S(2)}) collective-permute-start(bf16[80,4608]{1,0:T(8,128)(2,1)S(1)} %get-tuple-element.37), channel_id=1, source_target_pairs={{0,2},{2,4},{4,6},{6,8},{8,10},{10,12},{12,14},{14,16},{16,18},{18... | collective-permute-start | bytes 2211848 | tf_op jit(solution)/shard_map/ppermute | solution.py:242
  27.5 1.9 %collective-permute-start.3 = (bf16[80,4608]{1,0:T(8,128)(2,1)S(1)}, bf16[80,4608]{1,0:T(8,128)(2,1)S(1)}, u32[]{:S(2)}, u32[]{:S(2)}) collective-permute-start(bf16[80,4608]{1,0:T(8,128)(2,1)S(1)} %get-tuple-element.38), channel_id=1, source_target_pairs={{2,0},{4,2},{6,4},{8,6},{10,8},{12,10},{14,12},{16,14},{18,16},{20... | collective-permute-start | bytes 2211848 | tf_op jit(solution)/shard_map/ppermute | solution.py:242
  29.4 11.9 %collective-permute-done.4.refs_0_ = bf16[112,4608]{1,0:T(8,128)(2,1)} collective-permute-done((bf16[112,4608]{1,0:T(8,128)(2,1)}, bf16[112,4608]{1,0:T(8,128)(2,1)}, u32[]{:S(2)}, u32[]{:S(2)}) %collective-permute-start.4) | collective-permute-done | bytes 1032224 | tf_op jit(solution)/shard_map/ppermute | solution.py:242
  41.3 1.9 %collective-permute-done.5.refs_2_ = bf16[112,4608]{1,0:T(8,128)(2,1)} collective-permute-done((bf16[112,4608]{1,0:T(8,128)(2,1)}, bf16[112,4608]{1,0:T(8,128)(2,1)}, u32[]{:S(2)}, u32[]{:S(2)}) %collective-permute-start.5) | collective-permute-done | bytes 1032224 | tf_op jit(solution)/shard_map/ppermute | solution.py:242
  45.1 5.0 %collective-permute-start.7 = (bf16[96,4608]{1,0:T(8,128)(2,1)S(1)}, bf16[96,4608]{1,0:T(8,128)(2,1)S(1)}, u32[]{:S(2)}, u32[]{:S(2)}) collective-permute-start(bf16[96,4608]{1,0:T(8,128)(2,1)S(1)} %get-tuple-element.33), channel_id=1, source_target_pairs={{0,2},{2,4},{4,6},{6,8},{8,10},{10,12},{12,14},{14,16},{16,18},{18... | collective-permute-start | bytes 2654216 | tf_op jit(solution)/shard_map/ppermute | solution.py:242
  50.1 1.9 %collective-permute-start.8 = (bf16[96,4608]{1,0:T(8,128)(2,1)S(1)}, bf16[96,4608]{1,0:T(8,128)(2,1)S(1)}, u32[]{:S(2)}, u32[]{:S(2)}) collective-permute-start(bf16[96,4608]{1,0:T(8,128)(2,1)S(1)} %get-tuple-element.34), channel_id=1, source_target_pairs={{2,0},{4,2},{6,4},{8,6},{10,8},{12,10},{14,12},{16,14},{18,16},{20... | collective-permute-start | bytes 2654216 | tf_op jit(solution)/shard_map/ppermute | solution.py:242
  52.0 8.1 %products.5 = s32[80,2688]{1,0:T(8,128)S(1)} custom-call(s32[360]{0:T(512)S(1)} %reshape.8.index_ref, bf16[80,4608]{1,0:T(8,128)(2,1)S(1)} %collective-permute-done.2.refs_0_, bf16[80,5120]{1,0:T(8,128)(2,1)S(1)} %collective-permute-done.1.refs_1_, bf16[80,4608]{1,0:T(8,128)(2,1)S(1)} %collective-permute-done.3.refs_2_, bf16[40,9,128,128]{3,2,1,0:T(8,128)(2,1)} %refs_3_.9), custom_call_target="tpu_custom_call" | custom-call | flops 1 | bytes 1 | tf_op jit(solution)/shard_map/products/pallas_call | solution.py:133
  61.4 7.7 %products.6.own_ref = f32[112,5120]{1,0:T(8,128)S(1)} custom-call(s32[360]{0:T(512)S(1)} %reshape.8.index_ref, bf16[112,4608]{1,0:T(8,128)(2,1)} %collective-permute-done.4.refs_0_, bf16[256,5120]{1,0:T(8,128)(2,1)S(1)} %copy-done, bf16[112,4608]{1,0:T(8,128)(2,1)} %collective-permute-done.5.refs_2_, bf16[40,9,128,128]{3,2,1,0:T(8,128)(2,1)} %refs_3_.9), custom_call_target="tpu_custom_call" | custom-call | flops 1 | bytes 1 | tf_op jit(solution)/shard_map/products/pallas_call | solution.py:133
  69.3 3.9 %collective-permute-start.13 = (bf16[80,4608]{1,0:T(8,128)(2,1)S(1)}, bf16[80,4608]{1,0:T(8,128)(2,1)S(1)}, u32[]{:S(2)}, u32[]{:S(2)}) collective-permute-start(bf16[80,4608]{1,0:T(8,128)(2,1)S(1)} %get-tuple-element.21), channel_id=1, source_target_pairs={{0,2},{2,4},{4,6},{6,8},{8,10},{10,12},{12,14},{14,16},{16,18},{18... | collective-permute-start | bytes 2211848 | tf_op jit(solution)/shard_map/ppermute | solution.py:242
  73.2 1.9 %collective-permute-start.14 = (bf16[80,4608]{1,0:T(8,128)(2,1)S(1)}, bf16[80,4608]{1,0:T(8,128)(2,1)S(1)}, u32[]{:S(2)}, u32[]{:S(2)}) collective-permute-start(bf16[80,4608]{1,0:T(8,128)(2,1)S(1)} %get-tuple-element.22), channel_id=1, source_target_pairs={{2,0},{4,2},{6,4},{8,6},{10,8},{12,10},{14,12},{16,14},{18,16},{20... | collective-permute-start | bytes 2211848 | tf_op jit(solution)/shard_map/ppermute | solution.py:242
  75.2 8.4 %products.7 = s32[96,2688]{1,0:T(8,128)S(1)} custom-call(s32[360]{0:T(512)S(1)} %reshape.8.index_ref, bf16[96,4608]{1,0:T(8,128)(2,1)S(1)} %collective-permute-done.7.refs_0_, bf16[96,5120]{1,0:T(8,128)(2,1)} %collective-permute-done.refs_1_, bf16[96,4608]{1,0:T(8,128)(2,1)S(1)} %collective-permute-done.8.refs_2_, bf16[40,9,128,128]{3,2,1,0:T(8,128)(2,1)} %refs_3_.9), custom_call_target="tpu_custom_call" | custom-call | flops 1 | bytes 1 | tf_op jit(solution)/shard_map/products/pallas_call | solution.py:133
  85.7 3.9 %collective-permute-start.11 = (bf16[144,4608]{1,0:T(8,128)(2,1)S(1)}, bf16[144,4608]{1,0:T(8,128)(2,1)S(1)}, u32[]{:S(2)}, u32[]{:S(2)}) collective-permute-start(bf16[144,4608]{1,0:T(8,128)(2,1)S(1)} %get-tuple-element.26), channel_id=1, source_target_pairs={{0,2},{2,4},{4,6},{6,8},{8,10},{10,12},{12,14},{14,16},{16,18},{18... | collective-permute-start | bytes 3981320 | tf_op jit(solution)/shard_map/ppermute | solution.py:242
  89.6 1.9 %collective-permute-start.12 = (bf16[144,4608]{1,0:T(8,128)(2,1)S(1)}, bf16[144,4608]{1,0:T(8,128)(2,1)S(1)}, u32[]{:S(2)}, u32[]{:S(2)}) collective-permute-start(bf16[144,4608]{1,0:T(8,128)(2,1)S(1)} %get-tuple-element.27), channel_id=1, source_target_pairs={{2,0},{4,2},{6,4},{8,6},{10,8},{12,10},{14,12},{16,14},{18,16},{20... | collective-permute-start | bytes 3981320 | tf_op jit(solution)/shard_map/ppermute | solution.py:242
  91.5 8.1 %products.9 = s32[80,2688]{1,0:T(8,128)S(1)} custom-call(s32[360]{0:T(512)S(1)} %reshape.8.index_ref, bf16[80,4608]{1,0:T(8,128)(2,1)S(1)} %collective-permute-done.13.refs_0_, bf16[80,5120]{1,0:T(8,128)(2,1)S(1)} %collective-permute-done.6.refs_1_, bf16[80,4608]{1,0:T(8,128)(2,1)S(1)} %collective-permute-done.14.refs_2_, bf16[40,9,128,128]{3,2,1,0:T(8,128)(2,1)} %refs_3_.9), custom_call_target="tpu_custom_call" | custom-call | flops 1 | bytes 1 | tf_op jit(solution)/shard_map/products/pallas_call | solution.py:133
  99.6 7.2 %collective-permute-done.10.refs_0_.refs_1_ = s32[96,2688]{1,0:T(8,128)S(1)} collective-permute-done((s32[96,2688]{1,0:T(8,128)S(1)}, s32[96,2688]{1,0:T(8,128)S(1)}, u32[]{:S(2)}, u32[]{:S(2)}) %collective-permute-start.10) | collective-permute-done | bytes 1032224 | tf_op jit(solution)/shard_map/ppermute | solution.py:245
  108.0 10.5 %collective-permute-done.11.refs_0_ = bf16[144,4608]{1,0:T(8,128)(2,1)S(1)} collective-permute-done((bf16[144,4608]{1,0:T(8,128)(2,1)S(1)}, bf16[144,4608]{1,0:T(8,128)(2,1)S(1)}, u32[]{:S(2)}, u32[]{:S(2)}) %collective-permute-start.11) | collective-permute-done | bytes 1327136 | tf_op jit(solution)/shard_map/ppermute | solution.py:242
  118.5 2.6 %collective-permute-done.12.refs_2_ = bf16[144,4608]{1,0:T(8,128)(2,1)S(1)} collective-permute-done((bf16[144,4608]{1,0:T(8,128)(2,1)S(1)}, bf16[144,4608]{1,0:T(8,128)(2,1)S(1)}, u32[]{:S(2)}, u32[]{:S(2)}) %collective-permute-start.12) | collective-permute-done | bytes 1327136 | tf_op jit(solution)/shard_map/ppermute | solution.py:242
  121.1 7.2 %products.8.own_ref = f32[144,5120]{1,0:T(8,128)S(1)} custom-call(s32[360]{0:T(512)S(1)} %reshape.8.index_ref, bf16[144,4608]{1,0:T(8,128)(2,1)S(1)} %collective-permute-done.11.refs_0_, bf16[256,5120]{1,0:T(8,128)(2,1)S(1)} %copy-done, bf16[144,4608]{1,0:T(8,128)(2,1)S(1)} %collective-permute-done.12.refs_2_, bf16[40,9,128,128]{3,2,1,0:T(8,128)(2,1)} %refs_3_.9), custom_call_target="tpu_custom_call" | custom-call | flops 1 | bytes 1 | tf_op jit(solution)/shard_map/products/pallas_call | solution.py:133
  128.3 2.6 %finish.5 = bf16[256,5120]{1,0:T(8,128)(2,1)} custom-call(f32[144,5120]{1,0:T(8,128)S(1)} %products.8.own_ref, s32[96,2688]{1,0:T(8,128)S(1)} %collective-permute-done.10.refs_0_.refs_1_, s32[96,2688]{1,0:T(8,128)S(1)} %collective-permute-done.10.refs_0_.refs_1_, ...), custom_call_target="tpu_custom_call", output_to_operand_aliasing={{}: (5, {})} | custom-call | flops 1 | bytes 1 | tf_op jit(solution)/shard_map/finish/pallas_call | solution.py:200
  (34 shorter events, 9.5 us)
Async XLA Ops:
  0.0 12.4 %copy-start = (bf16[256,5120]{1,0:T(8,128)(2,1)S(1)}, bf16[256,5120]{1,0:T(8,128)(2,1)}, u32[]{:S(2)}) copy-start(bf16[256,5120]{1,0:T(8,128)(2,1)} %refs_1_.3) | copy-start | bytes 7864324
  2.3 11.4 %copy-start.1 = (s32[40,9]{0,1:T(8,128)S(1)}, s32[40,9]{0,1:T(8,128)}, u32[]{:S(2)}) copy-start(s32[40,9]{0,1:T(8,128)} %param.6) | copy-start | bytes 4324
  2.3 11.4 %copy-start.2 = (s32[40]{0:T(128)S(1)}, s32[40]{0:T(128)}, u32[]{:S(2)}) copy-start(s32[40]{0:T(128)} %param.7) | copy-start | bytes 484
  2.3 19.4 %collective-permute-start.1 = (bf16[80,5120]{1,0:T(8,128)(2,1)}, bf16[80,5120]{1,0:T(8,128)(2,1)S(1)}, u32[]{:S(2)}, u32[]{:S(2)}) collective-permute-start(bf16[80,5120]{1,0:T(8,128)(2,1)} %slice.50), channel_id=1, source_target_pairs={{0,1},{1,0},{2,3},{3,2},{4,5},{5,4},{6,7},{7,6},{8,9},{9,8},{10,11... | collective-permute-start | bytes 2457608 | tf_op jit(solution)/shard_map/ppermute | solution.py:245
  6.5 34.8 %collective-permute-start.4 = (bf16[112,4608]{1,0:T(8,128)(2,1)}, bf16[112,4608]{1,0:T(8,128)(2,1)}, u32[]{:S(2)}, u32[]{:S(2)}) collective-permute-start(bf16[112,4608]{1,0:T(8,128)(2,1)} %get-tuple-element.31), channel_id=1, source_target_pairs={{0,2},{2,4},{4,6},{6,8},{8,10},{10,12},{12,14},{14,16},{16,18},{18... | collective-permute-start | bytes 3096584 | tf_op jit(solution)/shard_map/ppermute | solution.py:242
  10.5 32.7 %collective-permute-start.5 = (bf16[112,4608]{1,0:T(8,128)(2,1)}, bf16[112,4608]{1,0:T(8,128)(2,1)}, u32[]{:S(2)}, u32[]{:S(2)}) collective-permute-start(bf16[112,4608]{1,0:T(8,128)(2,1)} %get-tuple-element.32), channel_id=1, source_target_pairs={{2,0},{4,2},{6,4},{8,6},{10,8},{12,10},{14,12},{16,14},{18,16},{20... | collective-permute-start | bytes 3096584 | tf_op jit(solution)/shard_map/ppermute | solution.py:242
  13.4 30.1 %collective-permute-start = (bf16[96,5120]{1,0:T(8,128)(2,1)}, bf16[96,5120]{1,0:T(8,128)(2,1)}, u32[]{:S(2)}, u32[]{:S(2)}) collective-permute-start(bf16[96,5120]{1,0:T(8,128)(2,1)} %slice.47), channel_id=1, source_target_pairs={{0,1},{1,0},{2,3},{3,2},{4,5},{5,4},{6,7},{7,6},{8,9},{9,8},{10,11... | collective-permute-start | bytes 2949128 | tf_op jit(solution)/shard_map/ppermute | solution.py:245
  21.8 30.2 %collective-permute-start.2 = (bf16[80,4608]{1,0:T(8,128)(2,1)S(1)}, bf16[80,4608]{1,0:T(8,128)(2,1)S(1)}, u32[]{:S(2)}, u32[]{:S(2)}) collective-permute-start(bf16[80,4608]{1,0:T(8,128)(2,1)S(1)} %get-tuple-element.37), channel_id=1, source_target_pairs={{0,2},{2,4},{4,6},{6,8},{8,10},{10,12},{12,14},{14,16},{16,18},{18... | collective-permute-start | bytes 2211848 | tf_op jit(solution)/shard_map/ppermute | solution.py:242
  27.5 24.6 %collective-permute-start.3 = (bf16[80,4608]{1,0:T(8,128)(2,1)S(1)}, bf16[80,4608]{1,0:T(8,128)(2,1)S(1)}, u32[]{:S(2)}, u32[]{:S(2)}) collective-permute-start(bf16[80,4608]{1,0:T(8,128)(2,1)S(1)} %get-tuple-element.38), channel_id=1, source_target_pairs={{2,0},{4,2},{6,4},{8,6},{10,8},{12,10},{14,12},{16,14},{18,16},{20... | collective-permute-start | bytes 2211848 | tf_op jit(solution)/shard_map/ppermute | solution.py:242
  43.2 26.0 %collective-permute-start.6 = (bf16[80,5120]{1,0:T(8,128)(2,1)S(1)}, bf16[80,5120]{1,0:T(8,128)(2,1)S(1)}, u32[]{:S(2)}, u32[]{:S(2)}) collective-permute-start(bf16[80,5120]{1,0:T(8,128)(2,1)S(1)} %slice.53), channel_id=1, source_target_pairs={{0,1},{1,0},{2,3},{3,2},{4,5},{5,4},{6,7},{7,6},{8,9},{9,8},{10,11... | collective-permute-start | bytes 2457608 | tf_op jit(solution)/shard_map/ppermute | solution.py:245
  45.1 30.1 %collective-permute-start.7 = (bf16[96,4608]{1,0:T(8,128)(2,1)S(1)}, bf16[96,4608]{1,0:T(8,128)(2,1)S(1)}, u32[]{:S(2)}, u32[]{:S(2)}) collective-permute-start(bf16[96,4608]{1,0:T(8,128)(2,1)S(1)} %get-tuple-element.33), channel_id=1, source_target_pairs={{0,2},{2,4},{4,6},{6,8},{8,10},{10,12},{12,14},{14,16},{16,18},{18... | collective-permute-start | bytes 2654216 | tf_op jit(solution)/shard_map/ppermute | solution.py:242
  50.1 25.1 %collective-permute-start.8 = (bf16[96,4608]{1,0:T(8,128)(2,1)S(1)}, bf16[96,4608]{1,0:T(8,128)(2,1)S(1)}, u32[]{:S(2)}, u32[]{:S(2)}) collective-permute-start(bf16[96,4608]{1,0:T(8,128)(2,1)S(1)} %get-tuple-element.34), channel_id=1, source_target_pairs={{2,0},{4,2},{6,4},{8,6},{10,8},{12,10},{14,12},{16,14},{18,16},{20... | collective-permute-start | bytes 2654216 | tf_op jit(solution)/shard_map/ppermute | solution.py:242
  60.1 23.5 %collective-permute-start.9 = (s32[80,2688]{1,0:T(8,128)S(1)}, s32[80,2688]{1,0:T(8,128)S(1)}, u32[]{:S(2)}, u32[]{:S(2)}) collective-permute-start(s32[80,2688]{1,0:T(8,128)S(1)} %products.5), channel_id=1, source_target_pairs={{0,1},{1,0},{2,3},{3,2},{4,5},{5,4},{6,7},{7,6},{8,9},{9,8},{10,11... | collective-permute-start | bytes 2580488 | tf_op jit(solution)/shard_map/ppermute | solution.py:245
  69.3 22.2 %collective-permute-start.13 = (bf16[80,4608]{1,0:T(8,128)(2,1)S(1)}, bf16[80,4608]{1,0:T(8,128)(2,1)S(1)}, u32[]{:S(2)}, u32[]{:S(2)}) collective-permute-start(bf16[80,4608]{1,0:T(8,128)(2,1)S(1)} %get-tuple-element.21), channel_id=1, source_target_pairs={{0,2},{2,4},{4,6},{6,8},{8,10},{10,12},{12,14},{14,16},{16,18},{18... | collective-permute-start | bytes 2211848 | tf_op jit(solution)/shard_map/ppermute | solution.py:242
  73.2 18.3 %collective-permute-start.14 = (bf16[80,4608]{1,0:T(8,128)(2,1)S(1)}, bf16[80,4608]{1,0:T(8,128)(2,1)S(1)}, u32[]{:S(2)}, u32[]{:S(2)}) collective-permute-start(bf16[80,4608]{1,0:T(8,128)(2,1)S(1)} %get-tuple-element.22), channel_id=1, source_target_pairs={{2,0},{4,2},{6,4},{8,6},{10,8},{12,10},{14,12},{16,14},{18,16},{20... | collective-permute-start | bytes 2211848 | tf_op jit(solution)/shard_map/ppermute | solution.py:242
  83.7 23.1 %collective-permute-start.10 = (s32[96,2688]{1,0:T(8,128)S(1)}, s32[96,2688]{1,0:T(8,128)S(1)}, u32[]{:S(2)}, u32[]{:S(2)}) collective-permute-start(s32[96,2688]{1,0:T(8,128)S(1)} %products.7), channel_id=1, source_target_pairs={{0,1},{1,0},{2,3},{3,2},{4,5},{5,4},{6,7},{7,6},{8,9},{9,8},{10,11... | collective-permute-start | bytes 3096584 | tf_op jit(solution)/shard_map/ppermute | solution.py:245
  85.7 32.8 %collective-permute-start.11 = (bf16[144,4608]{1,0:T(8,128)(2,1)S(1)}, bf16[144,4608]{1,0:T(8,128)(2,1)S(1)}, u32[]{:S(2)}, u32[]{:S(2)}) collective-permute-start(bf16[144,4608]{1,0:T(8,128)(2,1)S(1)} %get-tuple-element.26), channel_id=1, source_target_pairs={{0,2},{2,4},{4,6},{6,8},{8,10},{10,12},{12,14},{14,16},{16,18},{18... | collective-permute-start | bytes 3981320 | tf_op jit(solution)/shard_map/ppermute | solution.py:242
  89.6 31.5 %collective-permute-start.12 = (bf16[144,4608]{1,0:T(8,128)(2,1)S(1)}, bf16[144,4608]{1,0:T(8,128)(2,1)S(1)}, u32[]{:S(2)}, u32[]{:S(2)}) collective-permute-start(bf16[144,4608]{1,0:T(8,128)(2,1)S(1)} %get-tuple-element.27), channel_id=1, source_target_pairs={{2,0},{4,2},{6,4},{8,6},{10,8},{12,10},{14,12},{16,14},{18,16},{20... | collective-permute-start | bytes 3981320 | tf_op jit(solution)/shard_map/ppermute | solution.py:242
  106.8 21.5 %collective-permute-start.15 = (s32[80,2688]{1,0:T(8,128)S(1)}, s32[80,2688]{1,0:T(8,128)S(1)}, u32[]{:S(2)}, u32[]{:S(2)}) collective-permute-start(s32[80,2688]{1,0:T(8,128)S(1)} %products.9), channel_id=1, source_target_pairs={{0,1},{1,0},{2,3},{3,2},{4,5},{5,4},{6,7},{7,6},{8,9},{9,8},{10,11... | collective-permute-start | bytes 2580488 | tf_op jit(solution)/shard_map/ppermute | solution.py:245
